TPU v7x, 32 devices: a whole 2x2x4 slice. The times are simulated.
32 devices in a mesh: loop: 4 (over z), rep: 4 (over y, x), sec: 2 (over core).
Axes of the slice: x: 2, y: 2, z: 4, core: 2. Of those that a mesh axis runs over, the one named last changes fastest.
Arguments:
- student: bfloat16 [3072, 1024], P(('loop', 'rep'), 'sec'), may hold values from -6 to 6
- teacher: bfloat16 [3072, 4096], P(('loop', 'rep'), 'sec'), may hold values from -6 to 6
Outputs:
- student_grad: float32 [3072, 1024], P(('loop', 'rep'), 'sec')
All inputs are finite; a program needn't handle non-finite values.
Results may differ from a plain program's by a relative error of at most 0.022.
Values may be sent and summed in bfloat16 or wider, within the bound.
A program may use at most 128 MiB of HBM per device.

v0:
```python
import math

import jax
import jax.numpy as jnp
from jax import lax
from jax.sharding import PartitionSpec as P

DS = 1024


def passed_along(array, axis, by):
    length = lax.axis_size(axis)
    return lax.ppermute(array, axis, [(i, (i + by) % length) for i in range(length)])


def rows_product(left, right):
    return lax.dot_general(
        left, right, (((1,), (1,)), ((), ())), preferred_element_type=jnp.float32
    )


def body(student, teacher):
    eps = 1e-06
    rows = student.shape[0]
    loops = lax.axis_size("loop")
    half = loops // 2
    passages = rows * lax.axis_size("rep") * loops
    coef = 32.0 * DS / math.sqrt(passages)
    s32 = student.astype(jnp.float32)
    t32 = teacher.astype(jnp.float32)
    ssq_s, ssq_t = lax.psum((jnp.sum(s32 * s32, axis=1), jnp.sum(t32 * t32, axis=1)), "sec")
    inv_s = lax.rsqrt(ssq_s + eps)
    norm_s = (s32 * inv_s[:, None]).astype(jnp.bfloat16)
    norm_t = (t32 * lax.rsqrt(ssq_t + eps)[:, None]).astype(jnp.bfloat16)
    home_s, home_t = (
        lax.all_gather(norm_s, "rep", axis=0, tiled=True),
        lax.all_gather(norm_t, "rep", axis=0, tiled=True),
    )
    base_s, base_t = (norm_s, norm_t)
    visit_s = base_s
    visit_t = base_t
    carried = jnp.zeros((rows, base_s.shape[1]), jnp.float32)
    row_total = jnp.zeros((home_s.shape[0], base_s.shape[1]), jnp.float32)
    for step in range(half + 1):
        if step > 0:
            visit_s, visit_t = passed_along((visit_s, visit_t), "loop", 1)
        if step > 1:
            carried = passed_along(carried, "loop", 1)
        partial_tile = rows_product(home_s, visit_s) - rows_product(home_t, visit_t)
        tile = lax.psum(partial_tile, "sec").astype(jnp.bfloat16)
        row_total = row_total + jnp.dot(tile, visit_s, preferred_element_type=jnp.float32)
        if 0 < step < half:
            carried = carried + lax.dot_general(
                tile, home_s, (((0,), (0,)), ((), ())), preferred_element_type=jnp.float32
            )
    row_part = lax.psum_scatter(row_total, "rep", scatter_dimension=0, tiled=True)
    back = passed_along(carried, "loop", half)
    grad_n = coef * (row_part + back)
    norm_f = norm_s.astype(jnp.float32)
    inner = lax.psum(jnp.sum(grad_n * norm_f, axis=1), "sec")
    return (grad_n - inner[:, None] * norm_f) * inv_s[:, None]


def solution(mesh):
    placed = (P(("loop", "rep"), "sec"), P(("loop", "rep"), "sec"))
    return jax.shard_map(
        body, mesh=mesh, in_specs=placed, out_specs=P(("loop", "rep"), "sec"), check_vma=False
    )
```

profile of v0, /device:TPU:0, one launch (start us, length us, event | category | flops | bytes accessed | tf_op | source)
XLA Modules:
  0.0 130.3 jit_solution(11907605710414106803)
XLA Ops:
  6.5 1.0 fusion.2
  7.6 1.4 %fusion = f32[192]{0:T(256)S(1)} fusion(bf16[192,2048]{1,0:T(8,128)(2,1)} %param.3), kind=kLoop, calls=%fused_computation.2 | loop fusion | flops 1179456 | bytes 787200 | tf_op jit(solution)/shard_map/reduce_sum | solution.py:31
  9.0 2.6 %all-reduce.1 = (f32[192]{0:T(256)S(1)}, f32[192]{0:T(256)S(1)}) all-reduce(f32[192]{0:T(256)S(1)} %fusion.2, f32[192]{0:T(256)S(1)} %fusion), channel_id=1, replica_groups=mesh['loop'=4,'rep'=4,'sec'=2] {'sec'}, use_global_device_ids=true, to_apply=%region_1.0 | all-reduce | flops 384 | bytes 3072 | tf_op jit(solution)/shard_map/psum | solution.py:31
  11.6 2.2 %fusion.1 = bf16[192,2048]{1,0:T(8,128)(2,1)} fusion(bf16[192,2048]{1,0:T(8,128)(2,1)} %param.3, f32[192]{0:T(256)S(1)} %add_rsqrt_fusion), kind=kLoop, calls=%fused_computation.3 | loop fusion | flops 1179648 | bytes 1573632 | tf_op jit(solution)/shard_map/convert_element_type | solution.py:34
  13.8 0.0 all-gather.2.cloned.1.call-update
  13.8 0.0 reduce-scatter.2.cloned.1.call-start
  13.9 3.0 %collective-permute-start.1 = (bf16[192,2048]{1,0:T(8,128)(2,1)}, bf16[192,2048]{1,0:T(8,128)(2,1)S(1)}, u32[]{:S(2)}, u32[]{:S(2)}) collective-permute-start(bf16[192,2048]{1,0:T(8,128)(2,1)} %fusion.1), channel_id=1, source_target_pairs={{0,8},{8,16},{16,24},{24,0},{1,9},{9,17},{17,25},{25,1},{2,10},{10... | collective-permute-start | bytes 2359304 | tf_op jit(solution)/shard_map/ppermute | solution.py:13
  16.9 0.1 fusion.3
  17.0 1.6 %collective-permute-start = (bf16[192,512]{1,0:T(8,128)(2,1)S(1)}, bf16[192,512]{1,0:T(8,128)(2,1)S(1)}, u32[]{:S(2)}, u32[]{:S(2)}) collective-permute-start(bf16[192,512]{1,0:T(8,128)(2,1)S(1)} %fusion.3), channel_id=1, source_target_pairs={{0,8},{8,16},{16,24},{24,0},{1,9},{9,17},{17,25},{25,1},{2,10},{10... | collective-permute-start | bytes 589832 | tf_op jit(solution)/shard_map/ppermute | solution.py:13
  18.6 15.7 %all_gather.6 = bf16[768,512]{1,0:T(8,128)(2,1)S(1)} all-gather(bf16[192,512]{1,0:T(8,128)(2,1)S(1)} %fusion.3), channel_id=1, replica_groups=mesh['loop'=4,'rep'=4,'sec'=2] {'rep'}, dimensions={0}, use_global_device_ids=true | all-gather | bytes 983040 | tf_op jit(solution)/shard_map/all_gather | solution.py:36
  34.3 6.9 %collective-permute-done = bf16[192,512]{1,0:T(8,128)(2,1)S(1)} collective-permute-done((bf16[192,512]{1,0:T(8,128)(2,1)S(1)}, bf16[192,512]{1,0:T(8,128)(2,1)S(1)}, u32[]{:S(2)}, u32[]{:S(2)}) %collective-permute-start) | collective-permute-done | bytes 196640 | tf_op jit(solution)/shard_map/ppermute | solution.py:13
  41.2 1.3 collective-permute-start.3
  42.5 19.6 %all-gather.2.cloned.1.call-done = bf16[768,2048]{1,0:T(8,128)(2,1)} async-done(((bf16[192,2048]{1,0:T(8,128)(2,1)}), bf16[768,2048]{1,0:T(8,128)(2,1)}) %all-gather.2.cloned.1.call-update) | async-done | bytes 3145744 | tf_op jit(solution)/shard_map/all_gather | solution.py:37
  62.1 3.0 %fusion.14 = f32[768,192]{1,0:T(8,128)S(1)} fusion(bf16[768,2048]{1,0:T(8,128)(2,1)} %all-gather.2.cloned.1.call-done, bf16[192,2048]{1,0:T(8,128)(2,1)S(1)} %copy-done), kind=kOutput, calls=%fused_computation.27 | convolution fusion | flops 603979776 | bytes 4521984 | tf_op jit(solution)/shard_map/dot_general | solution.py:17
  65.1 0.4 convolution_subtract_fusion.1
  65.6 1.2 fusion.15
  66.8 0.4 convolution_subtract_fusion.2
  67.2 2.1 %fusion.16 = f32[768,192]{1,0:T(8,128)S(1)} fusion(bf16[768,2048]{1,0:T(8,128)(2,1)S(1)} %copy-done.4, bf16[192,2048]{1,0:T(8,128)(2,1)} %collective-permute-done.3), kind=kOutput, calls=%fused_computation.29 | convolution fusion | flops 603979776 | bytes 4521984 | tf_op jit(solution)/shard_map/dot_general | solution.py:17
  69.4 1.3 %convolution_subtract_fusion = f32[768,192]{1,0:T(8,128)S(1)} fusion(f32[768,192]{1,0:T(8,128)S(1)} %fusion.16, bf16[768,512]{1,0:T(8,128)(2,1)S(1)} %all_gather.6, bf16[192,512]{1,0:T(8,128)(2,1)} %collective-permute-done.2), kind=kOutput, calls=%fused_computation.5 | convolution fusion | flops 151142400 | bytes 2162688 | tf_op jit(solution)/shard_map/dot_general | solution.py:17
  70.7 9.5 %all-reduce.3 = (bf16[768,192]{1,0:T(8,128)(2,1)}, bf16[768,192]{0,1:T(8,128)(2,1)}, bf16[768,192]{1,0:T(8,128)(2,1)}) all-reduce(f32[768,192]{1,0:T(8,128)S(1)} %convolution_subtract_fusion.1, f32[768,192]{0,1:T(8,128)S(1)} %convolution_subtract_fusion.2, ...), channel_id=1, replica_groups=mesh['loop'=4,'rep'=4,'sec'=2] {'sec'}, use_global_device_ids=true, to_apply=%region_4.0 | all-reduce | flops 442368 | bytes 2654208 | tf_op jit(solution)/shard_map/psum | solution.py:50
  80.2 1.4 %fusion.17 = f32[768,512]{1,0:T(8,128)S(1)} fusion(bf16[768,192]{1,0:T(8,128)(2,1)} %get-tuple-element.5, bf16[192,512]{1,0:T(8,128)(2,1)S(1)} %fusion.3), kind=kOutput, calls=%fused_computation.30 | convolution fusion | flops 150994944 | bytes 2064384 | tf_op jit(solution)/shard_map/dot_general | solution.py:51
  81.6 0.4 fusion.19
  82.0 0.6 copy-done.3
  82.6 2.4 %add_add_fusion = f32[768,512]{1,0:T(8,128)} fusion(f32[768,512]{1,0:T(8,128)S(1)} %fusion.17, f32[768,512]{1,0:T(8,128)S(1)} %fusion.19, bf16[192,512]{1,0:T(8,128)(2,1)} %collective-permute-done.2, bf16[768,192]{1,0:T(8,128)(2,1)S(1)} %copy-done.3), kind=kOutput, calls=%fused_computation.4 | convolution fusion | flops 151781376 | bytes 5210112 | tf_op jit(solution)/shard_map/dot_general | solution.py:51
  85.0 0.3 fusion.18
  85.3 1.5 %collective-permute-start.4 = (f32[192,512]{1,0:T(8,128)S(1)}, f32[192,512]{1,0:T(8,128)S(1)}, u32[]{:S(2)}, u32[]{:S(2)}) collective-permute-start(f32[192,512]{1,0:T(8,128)S(1)} %fusion.18), channel_id=1, source_target_pairs={{0,8},{8,16},{16,24},{24,0},{1,9},{9,17},{17,25},{25,1},{2,10},{10... | collective-permute-start | bytes 1179656 | tf_op jit(solution)/shard_map/ppermute | solution.py:13
  86.9 11.8 %collective-permute-done.4 = f32[192,512]{1,0:T(8,128)S(1)} collective-permute-done((f32[192,512]{1,0:T(8,128)S(1)}, f32[192,512]{1,0:T(8,128)S(1)}, u32[]{:S(2)}, u32[]{:S(2)}) %collective-permute-start.4) | collective-permute-done | bytes 393248 | tf_op jit(solution)/shard_map/ppermute | solution.py:13
  98.6 0.6 collective-permute-start.5
  99.2 18.6 %collective-permute-done.5 = f32[192,512]{1,0:T(8,128)S(1)} collective-permute-done((f32[192,512]{1,0:T(8,128)S(1)}, f32[192,512]{1,0:T(8,128)S(1)}, u32[]{:S(2)}, u32[]{:S(2)}) %collective-permute-start.5) | collective-permute-done | bytes 393248 | tf_op jit(solution)/shard_map/ppermute | solution.py:13
  117.9 1.2 fusion.4
  119.1 2.5 %psum.47 = f32[192]{0:T(256)S(1)} all-reduce(f32[192]{0:T(256)S(1)} %fusion.4), channel_id=1, replica_groups=mesh['loop'=4,'rep'=4,'sec'=2] {'sec'}, use_global_device_ids=true, to_apply=%region_9.0 | all-reduce | flops 192 | bytes 1536 | tf_op jit(solution)/shard_map/psum | solution.py:60
  121.5 1.9 %fusion.6 = f32[192,512]{1,0:T(8,128)} fusion(f32[192]{0:T(256)S(1)} %psum.47, f32[192]{0:T(256)S(1)} %add_rsqrt_fusion.1, f32[192,512]{1,0:T(8,128)} %reduce-scatter.2.cloned.1.call-done, f32[192,512]{1,0:T(8,128)S(1)} %collective-permute-done.5, bf16[192,512]{1,0:T(8,128)(2,1)S(1)} %copy-done.1), kind=kLoop, calls=%fused_computation.16 | loop fusion | flops 884736 | bytes 1377792 | tf_op jit(solution)/shard_map/mul | solution.py:61
  (18 shorter events, 0.1 us)
Async XLA Ops:
  6.5 55.5 %all-gather.2.cloned.1.call-start = ((), (), s32[]{:S(2)}) async-start(), calls=%async_computation.1 | async-start | bytes 3932160 | tf_op jit(solution)/shard_map/all_gather | solution.py:37
  7.6 9.3 %copy-start.1 = (bf16[192,512]{1,0:T(8,128)(2,1)S(1)}, bf16[192,512]{1,0:T(8,128)(2,1)}, u32[]{:S(2)}) copy-start(bf16[192,512]{1,0:T(8,128)(2,1)} %param.2) | copy-start | bytes 589828
  13.8 48.3 %copy-start = (bf16[192,2048]{1,0:T(8,128)(2,1)S(1)}, bf16[192,2048]{1,0:T(8,128)(2,1)}, u32[]{:S(2)}) copy-start(bf16[192,2048]{1,0:T(8,128)(2,1)} %fusion.1) | copy-start | bytes 2359300
  13.8 104.0 %reduce-scatter.2.cloned.1.call-start = ((), (), s32[]{:S(2)}) async-start(), calls=%async_computation.2 | async-start | bytes 1966080 | tf_op jit(solution)/shard_map/reduce_scatter | solution.py:56
  13.9 27.3 %collective-permute-start.1 = (bf16[192,2048]{1,0:T(8,128)(2,1)}, bf16[192,2048]{1,0:T(8,128)(2,1)S(1)}, u32[]{:S(2)}, u32[]{:S(2)}) collective-permute-start(bf16[192,2048]{1,0:T(8,128)(2,1)} %fusion.1), channel_id=1, source_target_pairs={{0,8},{8,16},{16,24},{24,0},{1,9},{9,17},{17,25},{25,1},{2,10},{10... | collective-permute-start | bytes 2359304 | tf_op jit(solution)/shard_map/ppermute | solution.py:13
  17.0 24.2 %collective-permute-start = (bf16[192,512]{1,0:T(8,128)(2,1)S(1)}, bf16[192,512]{1,0:T(8,128)(2,1)S(1)}, u32[]{:S(2)}, u32[]{:S(2)}) collective-permute-start(bf16[192,512]{1,0:T(8,128)(2,1)S(1)} %fusion.3), channel_id=1, source_target_pairs={{0,8},{8,16},{16,24},{24,0},{1,9},{9,17},{17,25},{25,1},{2,10},{10... | collective-permute-start | bytes 589832 | tf_op jit(solution)/shard_map/ppermute | solution.py:13
  41.2 28.2 %collective-permute-start.2 = (bf16[192,512]{1,0:T(8,128)(2,1)S(1)}, bf16[192,512]{1,0:T(8,128)(2,1)}, u32[]{:S(2)}, u32[]{:S(2)}) collective-permute-start(bf16[192,512]{1,0:T(8,128)(2,1)S(1)} %collective-permute-done), channel_id=1, source_target_pairs={{0,8},{8,16},{16,24},{24,0},{1,9},{9,17},{17,25},{25,1},{2,10},{10... | collective-permute-start | bytes 589832 | tf_op jit(solution)/shard_map/ppermute | solution.py:13
  41.2 26.1 %collective-permute-start.3 = (bf16[192,2048]{1,0:T(8,128)(2,1)S(1)}, bf16[192,2048]{1,0:T(8,128)(2,1)}, u32[]{:S(2)}, u32[]{:S(2)}) collective-permute-start(bf16[192,2048]{1,0:T(8,128)(2,1)S(1)} %collective-permute-done.1), channel_id=1, source_target_pairs={{0,8},{8,16},{16,24},{24,0},{1,9},{9,17},{17,25},{25,1},{2,10},{10... | collective-permute-start | bytes 2359304 | tf_op jit(solution)/shard_map/ppermute | solution.py:13
  62.1 3.5 %copy-start.4 = (bf16[768,2048]{1,0:T(8,128)(2,1)S(1)}, bf16[768,2048]{1,0:T(8,128)(2,1)}, u32[]{:S(2)}) copy-start(bf16[768,2048]{1,0:T(8,128)(2,1)} %all-gather.2.cloned.1.call-done) | copy-start | bytes 9437188
  80.2 1.4 %copy-start.2 = (bf16[768,192]{0,1:T(8,128)(2,1)S(1)}, bf16[768,192]{0,1:T(8,128)(2,1)}, u32[]{:S(2)}) copy-start(bf16[768,192]{0,1:T(8,128)(2,1)} %get-tuple-element.6) | copy-start | bytes 884740
  81.6 1.0 copy-start.3
  85.3 13.3 %collective-permute-start.4 = (f32[192,512]{1,0:T(8,128)S(1)}, f32[192,512]{1,0:T(8,128)S(1)}, u32[]{:S(2)}, u32[]{:S(2)}) collective-permute-start(f32[192,512]{1,0:T(8,128)S(1)} %fusion.18), channel_id=1, source_target_pairs={{0,8},{8,16},{16,24},{24,0},{1,9},{9,17},{17,25},{25,1},{2,10},{10... | collective-permute-start | bytes 1179656 | tf_op jit(solution)/shard_map/ppermute | solution.py:13
  98.6 19.2 %collective-permute-start.5 = (f32[192,512]{1,0:T(8,128)S(1)}, f32[192,512]{1,0:T(8,128)S(1)}, u32[]{:S(2)}, u32[]{:S(2)}) collective-permute-start(f32[192,512]{1,0:T(8,128)S(1)} %collective-permute-done.4), channel_id=1, source_target_pairs={{0,16},{8,24},{16,0},{24,8},{1,17},{9,25},{17,1},{25,9},{2,18},{10... | collective-permute-start | bytes 1179656 | tf_op jit(solution)/shard_map/ppermute | solution.py:13
Sparse Core Ops, SparseCore 0:
  14.0 48.0 all-gather.1
  85.1 31.0 reduce-scatter.1
where the time goes:
time: 131 us; the launch traced here: 130 us
  waiting for transfers between devices  56.9 us (43%)
  blocking collectives  30.2 us (23%)
  between operations  13.5 us (10%)
  matrix products  13.1 us (10%)
  starting transfers between devices  8.06 us (6%)
  other arithmetic  7.93 us (6%)
    ppermute x6, waiting for transfers between devices, passed_along(): lax.ppermute(array, axis, [(i, (i + by) % length) for i in range(length)])  37.3 us
    all_gather x1, waiting for transfers between devices, body(): lax.all_gather(norm_t, 'rep', axis=0, tiled=True)  19.6 us
    all_gather x1, blocking collectives, body(): lax.all_gather(norm_s, 'rep', axis=0, tiled=True)  15.7 us
    psum x1, blocking collectives, body(): tile = lax.psum(partial_tile, 'sec').astype(jnp.bfloat16)  9.45 us
    dot_general x6, matrix products, rows_product(): lax.dot_general(left, right, (((1,), (1,)), ((), ())), preferred_element_...  8.55 us
    ppermute x6, starting transfers between devices, passed_along(): lax.ppermute(array, axis, [(i, (i + by) % length) for i in range(length)])  8.02 us
    dot_general x3, matrix products, body(): jnp.dot(tile, visit_s, preferred_element_type=jnp.float32)  4.21 us
  transfers between devices with their start and end apart: 8, of which 4 were waited for; matrix products, arithmetic and copies ran while one was open for 6% of the time, Pallas kernels for 0%

commit v1 on v0

v1 whole, which is shorter than its diff:
```python
import functools
import math

import jax
import jax.numpy as jnp
from jax import lax
from jax.experimental import pallas as pl
from jax.experimental.pallas import tpu as pltpu
from jax.sharding import PartitionSpec as P

MESH = pl.DeviceIdType.MESH
LANES = 128
PIECE = 256
LAG = 2
EPS = 1e-6


def kernel(
    loops, reps, coef, dup, s_ref, t_ref, out_ref,
    stat_tx, stat_rx, inv_keep, cols_all, feats, feats_tx, own, right_tx, left_tx,
    from_left, from_right, full, part_tx, part_rx, part_own, inner_tx, inner_rx,
    stat_sem, gather_send, gather_recv, swap_send, swap_recv,
    right_send, right_recv, left_send, left_recv, part_send, part_recv, inner_sem,
):
    z = lax.axis_index("loop")
    b = lax.axis_index("rep")
    c = lax.axis_index("sec")
    rows, width = s_ref.shape
    pieces, total_rows, _ = feats.shape
    t_own = (pieces - 1) // 2
    strips = width // LANES
    steps = strips * pieces
    sibling = (z, b, 1 - c)
    has_left = z > 0
    has_right = z < loops - 1

    def peer(d):
        return lax.rem(b + d, reps)

    def span(q):
        return pl.ds(pl.multiple_of(q * rows, rows), rows)

    barrier = pltpu.get_barrier_semaphore()
    for d in range(1, reps):
        pl.semaphore_signal(barrier, inc=1, device_id=(z, peer(d), c), device_id_type=MESH)
    pl.semaphore_signal(barrier, inc=1, device_id=sibling, device_id_type=MESH)

    @pl.when(has_left)
    def _():
        pl.semaphore_signal(barrier, inc=1, device_id=(z - 1, b, c), device_id_type=MESH)

    @pl.when(has_right)
    def _():
        pl.semaphore_signal(barrier, inc=1, device_id=(z + 1, b, c), device_id_type=MESH)

    s32 = s_ref[...].astype(jnp.float32)
    t32 = t_ref[...].astype(jnp.float32)
    part_s = jnp.sum(s32 * s32, axis=1, keepdims=True)
    part_t = jnp.sum(t32 * t32, axis=1, keepdims=True)
    lane = lax.broadcasted_iota(jnp.int32, (rows, LANES), 1)
    stat_tx[...] = jnp.where(lane < LANES // 2, part_s, part_t)

    pl.semaphore_wait(barrier, reps + has_left.astype(jnp.int32) + has_right.astype(jnp.int32))

    def remote(src, dst, send, recv, device):
        return pltpu.make_async_remote_copy(
            src_ref=src, dst_ref=dst, send_sem=send, recv_sem=recv,
            device_id=device, device_id_type=MESH,
        )

    stat = remote(stat_tx, stat_rx, stat_sem.at[0], stat_sem.at[1], sibling)
    stat.start()
    stat.wait()
    inv = lax.rsqrt(stat_tx[...] + stat_rx[...] + EPS)
    inv_s = inv[:, :1]
    inv_t = inv[:, LANES - 1:]
    inv_keep[...] = jnp.broadcast_to(inv_s, (rows, LANES))
    mine = span(b)
    cols_all[mine, :] = (s_ref[...].astype(jnp.float32) * inv_s).astype(jnp.bfloat16)

    def to_peer(d, kind):
        q = peer(d)
        if kind == 0:
            return remote(cols_all.at[mine], cols_all.at[mine],
                          gather_send.at[0, d], gather_recv.at[0, d], (z, q, c))
        return remote(feats_tx.at[q], feats.at[pl.ds(1, t_own), mine],
                      gather_send.at[1, d], gather_recv.at[1, d], (z, q, c))

    for d in range(1, reps):
        to_peer(d, 0).start()
    for q in range(reps):
        for p in range(t_own):
            lo = (q * t_own + p) * PIECE
            feats_tx[q, p] = (t_ref[:, lo:lo + PIECE].astype(jnp.float32) * inv_t).astype(jnp.bfloat16)
    for d in range(1, reps):
        to_peer(d, 1).start()
    for p in range(t_own):
        feats[1 + p, mine, :] = feats_tx[b, p]

    block = pl.ds(pl.multiple_of((b // dup) * LANES, LANES), LANES)

    def to_sibling(d, kind):
        at = span(lax.rem(b - d + reps, reps))
        if kind == 0:
            return remote(cols_all.at[at, block], feats.at[0, at, pl.ds(LANES, LANES)],
                          swap_send.at[0, d], swap_recv.at[0, d], sibling)
        return remote(feats.at[pl.ds(1, t_own), at], feats.at[pl.ds(1 + t_own, t_own), at],
                      swap_send.at[1, d], swap_recv.at[1, d], sibling)

    for kind in (0, 1):
        for d in range(reps):
            if d:
                to_peer(d, kind).wait_recv()
            to_sibling(d, kind).start()
    feats[0, :, :LANES] = cols_all[:, block]

    def product(p):
        value = lax.dot_general(
            feats[p], cols_all[...], (((0,), (0,)), ((), ())), preferred_element_type=jnp.float32
        )
        for j in range(strips):
            own[j * pieces + p] = value[:, j * LANES:(j + 1) * LANES]

    for p in range(1, 1 + t_own):
        product(p)
    for kind in (0, 1):
        for d in range(reps):
            to_sibling(d, kind).wait_recv()
    product(0)
    for p in range(1 + t_own, pieces):
        product(p)

    def rightward(k):
        return remote(right_tx.at[k], from_left.at[k], right_send.at[k], right_recv.at[k], (z + 1, b, c))

    def leftward(k):
        return remote(left_tx.at[k], from_right.at[k], left_send.at[k], left_recv.at[k], (z - 1, b, c))

    def result(j, d):
        return remote(part_tx.at[j, peer(d)], part_rx.at[j, d],
                      part_send.at[j, d], part_recv.at[j, d], (z, peer(d), c))

    def up(k):
        @pl.when(has_left)
        def _():
            rightward(k).wait_recv()

        @pl.when(has_right)
        def _():
            @pl.when(has_left)
            def _():
                right_tx[k] = (own[k] + from_left[k].astype(jnp.float32)).astype(jnp.bfloat16)

            @pl.when(jnp.logical_not(has_left))
            def _():
                right_tx[k] = own[k].astype(jnp.bfloat16)
            rightward(k).start()

    def down(k):
        @pl.when(has_right)
        def _():
            leftward(k).wait_recv()

        @pl.when(has_left)
        def _():
            @pl.when(has_right)
            def _():
                left_tx[k] = (own[k] + from_right[k].astype(jnp.float32)).astype(jnp.bfloat16)

            @pl.when(jnp.logical_not(has_right))
            def _():
                left_tx[k] = own[k].astype(jnp.bfloat16)
            leftward(k).start()

    def finish(k):
        j = k // pieces
        p = lax.rem(k, pieces)

        @pl.when(has_left)
        def _():
            own[k] = own[k] + from_left[k].astype(jnp.float32)

        @pl.when(has_right)
        def _():
            own[k] = own[k] + from_right[k].astype(jnp.float32)
        full[p] = own[k].astype(jnp.bfloat16)

        @pl.when(p == pieces - 1)
        def _():
            value = jnp.dot(feats[0], full[0], preferred_element_type=jnp.float32)
            if dup > 1:
                value = value * (1.0 / dup)
            for q in range(1, pieces):
                value = value - jnp.dot(feats[q], full[q], preferred_element_type=jnp.float32)
            for q in range(reps):
                part_tx[j, q] = value[q * rows:(q + 1) * rows].astype(jnp.bfloat16)

                @pl.when(b == q)
                def _():
                    part_own[j] = value[q * rows:(q + 1) * rows]
            for d in range(1, reps):
                result(j, d).start()

    lag_up = LAG * z
    lag_down = LAG * (loops - 1 - z)
    lag_end = jnp.maximum(lag_up, lag_down)

    def step(i, carry):
        for lag, act in ((lag_up, up), (lag_down, down), (lag_end, finish)):
            k = i - lag

            @pl.when(jnp.logical_and(k >= 0, k < steps))
            def _():
                act(k)
        return carry

    lax.fori_loop(0, steps + LAG * (loops - 1), step, 0)

    norm = cols_all[mine, :].astype(jnp.float32)
    inner = jnp.zeros((rows, 1), jnp.float32)
    grads = []
    for j in range(strips):
        grad = part_own[j]
        for d in range(1, reps):
            result(j, d).wait_recv()
            grad = grad + part_rx[j, d].astype(jnp.float32)
        grad = grad * coef
        grads.append(grad)
        inner = inner + jnp.sum(grad * norm[:, j * LANES:(j + 1) * LANES], axis=1, keepdims=True)
    inner_tx[...] = jnp.broadcast_to(inner, (rows, LANES))
    swap = remote(inner_tx, inner_rx, inner_sem.at[0], inner_sem.at[1], sibling)
    swap.start()
    swap.wait_recv()
    inner_all = inner_tx[...] + inner_rx[...]
    for j in range(strips):
        at = slice(j * LANES, (j + 1) * LANES)
        out_ref[:, at] = (grads[j] - inner_all * norm[:, at]) * inv_keep[...]

    swap.wait_send()
    for kind in (0, 1):
        for d in range(reps):
            if d:
                to_peer(d, kind).wait_send()
            to_sibling(d, kind).wait_send()
    for j in range(strips):
        for d in range(1, reps):
            result(j, d).wait_send()

    def drain(k, carry):
        @pl.when(has_right)
        def _():
            rightward(k).wait_send()

        @pl.when(has_left)
        def _():
            leftward(k).wait_send()
        return carry

    lax.fori_loop(0, steps, drain, 0)


def body(loops, reps, student, teacher):
    rows, width = student.shape
    passages = rows * reps * loops
    coef = 32.0 * (2 * width) / math.sqrt(passages)
    dup = max(1, reps * LANES // width)
    t_own = teacher.shape[1] // (reps * PIECE)
    pieces = 1 + 2 * t_own
    strips = width // LANES
    steps = strips * pieces
    total = rows * reps
    f32, bf16 = jnp.float32, jnp.bfloat16
    dma = pltpu.SemaphoreType.DMA
    flops = 4 * total * pieces * PIECE * width
    return pl.pallas_call(
        functools.partial(kernel, loops, reps, coef, dup),
        out_shape=jax.ShapeDtypeStruct((rows, width), f32),
        in_specs=[pl.BlockSpec(memory_space=pltpu.VMEM)] * 2,
        out_specs=pl.BlockSpec(memory_space=pltpu.VMEM),
        scratch_shapes=[
            pltpu.VMEM((rows, LANES), f32),
            pltpu.VMEM((rows, LANES), f32),
            pltpu.VMEM((rows, LANES), f32),
            pltpu.VMEM((total, width), bf16),
            pltpu.VMEM((pieces, total, PIECE), bf16),
            pltpu.VMEM((reps, t_own, rows, PIECE), bf16),
            pltpu.VMEM((steps, PIECE, LANES), f32),
            pltpu.VMEM((steps, PIECE, LANES), bf16),
            pltpu.VMEM((steps, PIECE, LANES), bf16),
            pltpu.VMEM((steps, PIECE, LANES), bf16),
            pltpu.VMEM((steps, PIECE, LANES), bf16),
            pltpu.VMEM((pieces, PIECE, LANES), bf16),
            pltpu.VMEM((strips, reps, rows, LANES), bf16),
            pltpu.VMEM((strips, reps, rows, LANES), bf16),
            pltpu.VMEM((strips, rows, LANES), f32),
            pltpu.VMEM((rows, LANES), f32),
            pltpu.VMEM((rows, LANES), f32),
            dma((2,)),
            dma((2, reps)),
            dma((2, reps)),
            dma((2, reps)),
            dma((2, reps)),
            dma((steps,)),
            dma((steps,)),
            dma((steps,)),
            dma((steps,)),
            dma((strips, reps)),
            dma((strips, reps)),
            dma((2,)),
        ],
        compiler_params=pltpu.CompilerParams(
            collective_id=0, has_side_effects=True, vmem_limit_bytes=48 * 1024 * 1024
        ),
        cost_estimate=pl.CostEstimate(flops=flops, bytes_accessed=4 * rows * width, transcendentals=0),
    )(student, teacher)


def solution(mesh):
    placed = P(("loop", "rep"), "sec")
    return jax.shard_map(
        functools.partial(body, mesh.shape["loop"], mesh.shape["rep"]),
        mesh=mesh, in_specs=(placed, placed), out_specs=placed, check_vma=False,
    )
```

time: 131 us -> 79.4 us (0.61)
  Pallas kernels: 0 us -> 76.4 us
  waiting for transfers between devices: 56.9 us -> 0 us
  blocking collectives: 30.2 us -> 0 us
  between operations: 13.5 us -> 0.01 us
  matrix products: 13.1 us -> 0 us
  starting transfers between devices: 8.06 us -> 0 us
  other arithmetic: 7.93 us -> 0 us
  local copies, waits for them, and re-layouts: 0.6 us -> 2.81 us
    pallas_call x0 -> x1, Pallas kernels: none -> 76.4 us  [body(): pl.pallas_call(functools.partial(kernel, loops, reps, coef, dup), out_sha...]
    ppermute x6 -> x0, waiting for transfers between devices: 37.3 us -> none  [passed_along(): lax.ppermute(array, axis, [(i, (i + by) % length) for i in range(length)])]
    all_gather x1 -> x0, waiting for transfers between devices: 19.6 us -> none  [body(): lax.all_gather(norm_t, 'rep', axis=0, tiled=True)]
    all_gather x1 -> x0, blocking collectives: 15.7 us -> none  [body(): lax.all_gather(norm_s, 'rep', axis=0, tiled=True)]
    psum x3 -> x0, blocking collectives: 14.5 us -> none  [the longest x1 9.45 us: body(): tile = lax.psum(partial_tile, 'sec').astype(jnp.bfloat16)]
    dot_general x10 -> x0, matrix products: 13.1 us -> none  [the longest x6 8.55 us: rows_product(): lax.dot_general(left, right, (((1,), (1,)), ((), ())), preferred_element_...]
    ppermute x6 -> x0, starting transfers between devices: 8.02 us -> none  [passed_along(): lax.ppermute(array, axis, [(i, (i + by) % length) for i in range(length)])]
    reduce_sum x3 -> x0, other arithmetic: 3.67 us -> none  [the longest x1 1.41 us: body(): jnp.sum(t32 * t32, axis=1)]
  transfers between devices with their start and end apart: 8 -> 0, of which waited for: 4 -> 0; matrix products, arithmetic and copies ran while one was open for 6% -> 0% of each run, Pallas kernels for 0% -> 0%
where the time goes in v1:
time: 79.4 us; the launch traced here: 79.3 us
  Pallas kernels  76.4 us (96%)
  local copies, waits for them, and re-layouts  2.81 us (4%)
    pallas_call x1, Pallas kernels, body(): pl.pallas_call(functools.partial(kernel, loops, reps, coef, dup), out_sha...  76.4 us
    unnamed x5, local copies, waits for them, and re-layouts  2.81 us

profile of v1, /device:TPU:0, one launch (start us, length us, event | category | flops | bytes accessed | tf_op | source)
XLA Modules:
  0.0 79.3 jit_solution(10433958581204203031)
XLA Ops:
  0.0 0.0 copy-start
  0.0 1.1 %copy-done = bf16[192,2048]{1,0:T(8,128)(2,1)S(1)} copy-done((bf16[192,2048]{1,0:T(8,128)(2,1)S(1)}, bf16[192,2048]{1,0:T(8,128)(2,1)}, u32[]{:S(2)}) %copy-start) | copy-done | bytes 786456
  1.1 0.0 copy-start.1
  1.1 0.9 %copy-done.1 = bf16[192,512]{1,0:T(8,128)(2,1)S(1)} copy-done((bf16[192,512]{1,0:T(8,128)(2,1)S(1)}, bf16[192,512]{1,0:T(8,128)(2,1)}, u32[]{:S(2)}) %copy-start.1) | copy-done | bytes 196632
  2.1 76.4 %shard_map.28 = f32[192,512]{1,0:T(8,128)S(1)} custom-call(bf16[192,512]{1,0:T(8,128)(2,1)S(1)} %copy-done.1, bf16[192,2048]{1,0:T(8,128)(2,1)S(1)} %copy-done), custom_call_target="tpu_custom_call" | custom-call | flops 2013265920 | bytes 393216 | tf_op jit(solution)/shard_map/pallas_call | solution.py:275
  78.5 0.7 copy.4
Async XLA Ops:
  0.0 1.1 %copy-start = (bf16[192,2048]{1,0:T(8,128)(2,1)S(1)}, bf16[192,2048]{1,0:T(8,128)(2,1)}, u32[]{:S(2)}) copy-start(bf16[192,2048]{1,0:T(8,128)(2,1)} %t_ref.1) | copy-start | bytes 2359300
  1.1 0.9 %copy-start.1 = (bf16[192,512]{1,0:T(8,128)(2,1)S(1)}, bf16[192,512]{1,0:T(8,128)(2,1)}, u32[]{:S(2)}) copy-start(bf16[192,512]{1,0:T(8,128)(2,1)} %s_ref.1) | copy-start | bytes 589828

commit v2 on v1

--- a/solution.py
+++ b/solution.py
@@ -11,15 +11,17 @@
 MESH = pl.DeviceIdType.MESH
 LANES = 128
 PIECE = 256
-LAG = 2
+LAG = 3
+EARLY = 2
+IDLE = 4
 EPS = 1e-6
 
 
 def kernel(
-    loops, reps, coef, dup, s_ref, t_ref, out_ref,
-    stat_tx, stat_rx, inv_keep, cols_all, feats, feats_tx, own, right_tx, left_tx,
+    loops, reps, coef, dup, s_hbm, t_hbm, out_ref,
+    s_ref, t_ref, stat_tx, stat_rx, inv_keep, cols_all, cols_t, feats, feats_tx, own, right_tx, left_tx,
     from_left, from_right, full, part_tx, part_rx, part_own, inner_tx, inner_rx,
-    stat_sem, gather_send, gather_recv, swap_send, swap_recv,
+    load_sem, stat_sem, strip_send, strip_recv, gather_send, gather_recv, swap_send, swap_recv,
     right_send, right_recv, left_send, left_recv, part_send, part_recv, inner_sem,
 ):
     z = lax.axis_index("loop")
@@ -40,6 +42,13 @@
     def span(q):
         return pl.ds(pl.multiple_of(q * rows, rows), rows)
 
+    def lanes(j):
+        return pl.ds(pl.multiple_of(j * LANES, LANES), LANES)
+
+    load_s = pltpu.make_async_copy(s_hbm, s_ref, load_sem.at[0])
+    load_t = pltpu.make_async_copy(t_hbm, t_ref, load_sem.at[1])
+    load_s.start()
+    load_t.start()
     barrier = pltpu.get_barrier_semaphore()
     for d in range(1, reps):
         pl.semaphore_signal(barrier, inc=1, device_id=(z, peer(d), c), device_id_type=MESH)
@@ -53,9 +62,11 @@
     def _():
         pl.semaphore_signal(barrier, inc=1, device_id=(z + 1, b, c), device_id_type=MESH)
 
+    load_s.wait()
     s32 = s_ref[...].astype(jnp.float32)
+    part_s = jnp.sum(s32 * s32, axis=1, keepdims=True)
+    load_t.wait()
     t32 = t_ref[...].astype(jnp.float32)
-    part_s = jnp.sum(s32 * s32, axis=1, keepdims=True)
     part_t = jnp.sum(t32 * t32, axis=1, keepdims=True)
     lane = lax.broadcasted_iota(jnp.int32, (rows, LANES), 1)
     stat_tx[...] = jnp.where(lane < LANES // 2, part_s, part_t)
@@ -78,57 +89,53 @@
     mine = span(b)
     cols_all[mine, :] = (s_ref[...].astype(jnp.float32) * inv_s).astype(jnp.bfloat16)
 
-    def to_peer(d, kind):
-        q = peer(d)
-        if kind == 0:
-            return remote(cols_all.at[mine], cols_all.at[mine],
-                          gather_send.at[0, d], gather_recv.at[0, d], (z, q, c))
-        return remote(feats_tx.at[q], feats.at[pl.ds(1, t_own), mine],
-                      gather_send.at[1, d], gather_recv.at[1, d], (z, q, c))
+    def strip_to(d, j):
+        at = lanes(j)
+        return remote(cols_all.at[mine, at], cols_all.at[mine, at],
+                      strip_send.at[j, d], strip_recv.at[j, d], (z, peer(d), c))
+
+    def piece_to(d, p):
+        return remote(feats_tx.at[peer(d), p], feats.at[2 * p, mine],
+                      gather_send.at[p, d], gather_recv.at[p, d], (z, peer(d), c))
 
     for d in range(1, reps):
-        to_peer(d, 0).start()
-    for q in range(reps):
-        for p in range(t_own):
+        strip_to(d, 0).start()
+    for p in range(t_own):
+        for q in range(reps):
             lo = (q * t_own + p) * PIECE
             feats_tx[q, p] = (t_ref[:, lo:lo + PIECE].astype(jnp.float32) * inv_t).astype(jnp.bfloat16)
-    for d in range(1, reps):
-        to_peer(d, 1).start()
-    for p in range(t_own):
-        feats[1 + p, mine, :] = feats_tx[b, p]
-
-    block = pl.ds(pl.multiple_of((b // dup) * LANES, LANES), LANES)
-
-    def to_sibling(d, kind):
-        at = span(lax.rem(b - d + reps, reps))
-        if kind == 0:
-            return remote(cols_all.at[at, block], feats.at[0, at, pl.ds(LANES, LANES)],
-                          swap_send.at[0, d], swap_recv.at[0, d], sibling)
-        return remote(feats.at[pl.ds(1, t_own), at], feats.at[pl.ds(1 + t_own, t_own), at],
-                      swap_send.at[1, d], swap_recv.at[1, d], sibling)
-
-    for kind in (0, 1):
-        for d in range(reps):
-            if d:
-                to_peer(d, kind).wait_recv()
-            to_sibling(d, kind).start()
-    feats[0, :, :LANES] = cols_all[:, block]
-
-    def product(p):
-        value = lax.dot_general(
-            feats[p], cols_all[...], (((0,), (0,)), ((), ())), preferred_element_type=jnp.float32
-        )
-        for j in range(strips):
-            own[j * pieces + p] = value[:, j * LANES:(j + 1) * LANES]
-
-    for p in range(1, 1 + t_own):
-        product(p)
-    for kind in (0, 1):
-        for d in range(reps):
-            to_sibling(d, kind).wait_recv()
-    product(0)
-    for p in range(1 + t_own, pieces):
-        product(p)
+        for d in range(1, reps):
+            piece_to(d, p).start()
+        feats[2 * p, mine, :] = feats_tx[b, p]
+    for m in range(strips):
+        for d in range(1, reps):
+            j = lax.rem(peer(d) // dup + m, strips)
+
+            @pl.when(j > 0)
+            def _():
+                strip_to(d, j).start()
+
+    block = b // dup
+
+    def came(d):
+        return span(lax.rem(b - d + reps, reps))
+
+    def piece_over(d, p):
+        at = came(d)
+        return remote(feats.at[2 * p, at], feats.at[2 * p + 1, at],
+                      swap_send.at[p, d], swap_recv.at[p, d], sibling)
+
+    def block_over(d):
+        at = came(d)
+        return remote(cols_all.at[at, lanes(block)], feats.at[pieces - 1, at, pl.ds(LANES, LANES)],
+                      swap_send.at[t_own, d], swap_recv.at[t_own, d], sibling)
+
+    def strip_in(j):
+        for d in range(1, reps):
+            strip_to(d, j).wait_recv()
+
+    def turn(j):
+        cols_t[j] = cols_all[:, j * LANES:(j + 1) * LANES].T
 
     def rightward(k):
         return remote(right_tx.at[k], from_left.at[k], right_send.at[k], right_recv.at[k], (z + 1, b, c))
@@ -140,6 +147,11 @@
         return remote(part_tx.at[j, peer(d)], part_rx.at[j, d],
                       part_send.at[j, d], part_recv.at[j, d], (z, peer(d), c))
 
+    def produce(k):
+        own[k] = jnp.dot(
+            cols_t[k // pieces], feats[lax.rem(k, pieces)], preferred_element_type=jnp.float32
+        )
+
     def up(k):
         @pl.when(has_left)
         def _():
@@ -171,6 +183,9 @@
             def _():
                 left_tx[k] = own[k].astype(jnp.bfloat16)
             leftward(k).start()
+
+    def across(left, right):
+        return lax.dot_general(left, right, (((1,), (1,)), ((), ())), preferred_element_type=jnp.float32)
 
     def finish(k):
         j = k // pieces
@@ -187,11 +202,11 @@
 
         @pl.when(p == pieces - 1)
         def _():
-            value = jnp.dot(feats[0], full[0], preferred_element_type=jnp.float32)
+            value = across(feats[pieces - 1], full[pieces - 1])
             if dup > 1:
                 value = value * (1.0 / dup)
-            for q in range(1, pieces):
-                value = value - jnp.dot(feats[q], full[q], preferred_element_type=jnp.float32)
+            for q in range(pieces - 1):
+                value = value - across(feats[q], full[q])
             for q in range(reps):
                 part_tx[j, q] = value[q * rows:(q + 1) * rows].astype(jnp.bfloat16)
 
@@ -205,16 +220,61 @@
     lag_down = LAG * (loops - 1 - z)
     lag_end = jnp.maximum(lag_up, lag_down)
 
-    def step(i, carry):
+    def chunk_at(i):
+        k = jnp.where(i < EARLY, i, i - IDLE)
+        idle = jnp.logical_and(i >= EARLY, i < EARLY + IDLE)
+        return k, jnp.logical_and(jnp.logical_not(idle), jnp.logical_and(i >= 0, k < steps))
+
+    def tick(i, carry):
         for lag, act in ((lag_up, up), (lag_down, down), (lag_end, finish)):
-            k = i - lag
-
-            @pl.when(jnp.logical_and(k >= 0, k < steps))
+            k, live = chunk_at(i - lag)
+
+            @pl.when(live)
             def _():
                 act(k)
         return carry
 
-    lax.fori_loop(0, steps + LAG * (loops - 1), step, 0)
+    def made(k):
+        produce(k)
+        tick(k if k < EARLY else k + IDLE, 0)
+
+    for p in range(t_own):
+        piece_over(0, p).start()
+    block_over(0).start()
+    strip_in(0)
+    turn(0)
+    for p in range(t_own):
+        for d in range(1, reps):
+            piece_to(d, p).wait_recv()
+            piece_over(d, p).start()
+        made(2 * p)
+        for d in range(reps):
+            piece_over(d, p).wait_recv()
+        made(2 * p + 1)
+        if p == 0:
+            lax.fori_loop(EARLY, EARLY + IDLE, tick, 0)
+
+    @pl.when(block > 0)
+    def _():
+        strip_in(block)
+    for d in range(1, reps):
+        block_over(d).start()
+    feats[pieces - 1, :, :LANES] = cols_all[:, lanes(block)]
+    for d in range(reps):
+        block_over(d).wait_recv()
+    made(pieces - 1)
+    for j in range(1, strips):
+        @pl.when(block != j)
+        def _():
+            strip_in(j)
+        turn(j)
+
+        def make(k, carry):
+            produce(k)
+            return tick(k + IDLE, carry)
+
+        lax.fori_loop(j * pieces, (j + 1) * pieces, make, 0)
+    lax.fori_loop(steps + IDLE, steps + IDLE + LAG * (loops - 1), tick, 0)
 
     norm = cols_all[mine, :].astype(jnp.float32)
     inner = jnp.zeros((rows, 1), jnp.float32)
@@ -237,13 +297,15 @@
         out_ref[:, at] = (grads[j] - inner_all * norm[:, at]) * inv_keep[...]
 
     swap.wait_send()
-    for kind in (0, 1):
-        for d in range(reps):
+    for d in range(reps):
+        for p in range(t_own):
+            piece_over(d, p).wait_send()
             if d:
-                to_peer(d, kind).wait_send()
-            to_sibling(d, kind).wait_send()
+                piece_to(d, p).wait_send()
+        block_over(d).wait_send()
     for j in range(strips):
         for d in range(1, reps):
+            strip_to(d, j).wait_send()
             result(j, d).wait_send()
 
     def drain(k, carry):
@@ -275,31 +337,37 @@
     return pl.pallas_call(
         functools.partial(kernel, loops, reps, coef, dup),
         out_shape=jax.ShapeDtypeStruct((rows, width), f32),
-        in_specs=[pl.BlockSpec(memory_space=pltpu.VMEM)] * 2,
+        in_specs=[pl.BlockSpec(memory_space=pltpu.HBM)] * 2,
         out_specs=pl.BlockSpec(memory_space=pltpu.VMEM),
         scratch_shapes=[
+            pltpu.VMEM((rows, width), bf16),
+            pltpu.VMEM((rows, teacher.shape[1]), bf16),
             pltpu.VMEM((rows, LANES), f32),
             pltpu.VMEM((rows, LANES), f32),
             pltpu.VMEM((rows, LANES), f32),
             pltpu.VMEM((total, width), bf16),
+            pltpu.VMEM((strips, LANES, total), bf16),
             pltpu.VMEM((pieces, total, PIECE), bf16),
             pltpu.VMEM((reps, t_own, rows, PIECE), bf16),
-            pltpu.VMEM((steps, PIECE, LANES), f32),
-            pltpu.VMEM((steps, PIECE, LANES), bf16),
-            pltpu.VMEM((steps, PIECE, LANES), bf16),
-            pltpu.VMEM((steps, PIECE, LANES), bf16),
-            pltpu.VMEM((steps, PIECE, LANES), bf16),
-            pltpu.VMEM((pieces, PIECE, LANES), bf16),
+            pltpu.VMEM((steps, LANES, PIECE), f32),
+            pltpu.VMEM((steps, LANES, PIECE), bf16),
+            pltpu.VMEM((steps, LANES, PIECE), bf16),
+            pltpu.VMEM((steps, LANES, PIECE), bf16),
+            pltpu.VMEM((steps, LANES, PIECE), bf16),
+            pltpu.VMEM((pieces, LANES, PIECE), bf16),
             pltpu.VMEM((strips, reps, rows, LANES), bf16),
             pltpu.VMEM((strips, reps, rows, LANES), bf16),
             pltpu.VMEM((strips, rows, LANES), f32),
             pltpu.VMEM((rows, LANES), f32),
             pltpu.VMEM((rows, LANES), f32),
             dma((2,)),
-            dma((2, reps)),
-            dma((2, reps)),
-            dma((2, reps)),
-            dma((2, reps)),
+            dma((2,)),
+            dma((strips, reps)),
+            dma((strips, reps)),
+            dma((t_own, reps)),
+            dma((t_own, reps)),
+            dma((t_own + 1, reps)),
+            dma((t_own + 1, reps)),
             dma((steps,)),
             dma((steps,)),
             dma((steps,)),

time: 79.4 us -> 67 us (0.84)
  Pallas kernels: 76.4 us -> 64 us
    pallas_call x1, Pallas kernels: 76.4 us -> 64 us  [body(): pl.pallas_call(functools.partial(kernel, loops, reps, coef, dup), out_sha...]
where the time goes in v2:
time: 67 us; the launch traced here: 66.9 us
  Pallas kernels  64 us (96%)
  local copies, waits for them, and re-layouts  2.81 us (4%)
    pallas_call x1, Pallas kernels, body(): pl.pallas_call(functools.partial(kernel, loops, reps, coef, dup), out_sha...  64 us
    unnamed x5, local copies, waits for them, and re-layouts  2.81 us

profile of v2, /device:TPU:0, one launch (start us, length us, event | category | flops | bytes accessed | tf_op | source)
XLA Modules:
  0.0 66.9 jit_solution(7332931438815967313)
XLA Ops:
  0.0 0.0 copy-start
  0.0 1.1 %copy-done = bf16[192,2048]{1,0:T(8,128)(2,1)S(1)} copy-done((bf16[192,2048]{1,0:T(8,128)(2,1)S(1)}, bf16[192,2048]{1,0:T(8,128)(2,1)}, u32[]{:S(2)}) %copy-start) | copy-done | bytes 786456
  1.1 0.0 copy-start.1
  1.1 0.9 %copy-done.1 = bf16[192,512]{1,0:T(8,128)(2,1)S(1)} copy-done((bf16[192,512]{1,0:T(8,128)(2,1)S(1)}, bf16[192,512]{1,0:T(8,128)(2,1)}, u32[]{:S(2)}) %copy-start.1) | copy-done | bytes 196632
  2.1 64.0 %shard_map.28 = f32[192,512]{1,0:T(8,128)S(1)} custom-call(bf16[192,512]{1,0:T(8,128)(2,1)S(1)} %copy-done.1, bf16[192,2048]{1,0:T(8,128)(2,1)S(1)} %copy-done), custom_call_target="tpu_custom_call" | custom-call | flops 2013265920 | bytes 393216 | tf_op jit(solution)/shard_map/pallas_call | solution.py:337
  66.1 0.7 %copy.4 = f32[192,512]{1,0:T(8,128)} copy(f32[192,512]{1,0:T(8,128)S(1)} %shard_map.28) | data formatting | bytes 786432
Async XLA Ops:
  0.0 1.1 %copy-start = (bf16[192,2048]{1,0:T(8,128)(2,1)S(1)}, bf16[192,2048]{1,0:T(8,128)(2,1)}, u32[]{:S(2)}) copy-start(bf16[192,2048]{1,0:T(8,128)(2,1)} %t_hbm.1) | copy-start | bytes 2359300
  1.1 0.9 %copy-start.1 = (bf16[192,512]{1,0:T(8,128)(2,1)S(1)}, bf16[192,512]{1,0:T(8,128)(2,1)}, u32[]{:S(2)}) copy-start(bf16[192,512]{1,0:T(8,128)(2,1)} %s_hbm.1) | copy-start | bytes 589828

commit v3 on v2

--- a/solution.py
+++ b/solution.py
@@ -104,10 +104,12 @@
         for q in range(reps):
             lo = (q * t_own + p) * PIECE
             feats_tx[q, p] = (t_ref[:, lo:lo + PIECE].astype(jnp.float32) * inv_t).astype(jnp.bfloat16)
-        for d in range(1, reps):
-            piece_to(d, p).start()
+        if p == 0:
+            for d in range(1, reps):
+                piece_to(d, 0).start()
         feats[2 * p, mine, :] = feats_tx[b, p]
-    for m in range(strips):
+
+    def send_strips(m):
         for d in range(1, reps):
             j = lax.rem(peer(d) // dup + m, strips)
 
@@ -242,11 +244,19 @@
         piece_over(0, p).start()
     block_over(0).start()
     strip_in(0)
+    for p in range(1, t_own):
+        for d in range(1, reps):
+            piece_to(d, p).start()
     turn(0)
     for p in range(t_own):
         for d in range(1, reps):
             piece_to(d, p).wait_recv()
             piece_over(d, p).start()
+        if p == 0:
+            send_strips(0)
+        if p == t_own - 1:
+            for m in range(1, strips):
+                send_strips(m)
         made(2 * p)
         for d in range(reps):
             piece_over(d, p).wait_recv()
@@ -377,7 +387,7 @@
             dma((2,)),
         ],
         compiler_params=pltpu.CompilerParams(
-            collective_id=0, has_side_effects=True, vmem_limit_bytes=48 * 1024 * 1024
+            collective_id=0, has_side_effects=True, vmem_limit_bytes=64 * 1024 * 1024
         ),
         cost_estimate=pl.CostEstimate(flops=flops, bytes_accessed=4 * rows * width, transcendentals=0),
     )(student, teacher)

time: 67 us -> 68.1 us (1.016)
  Pallas kernels: 64 us -> 66.1 us
  local copies, waits for them, and re-layouts: 2.81 us -> 1.77 us
    pallas_call x1, Pallas kernels: 64 us -> 66.1 us  [body(): pl.pallas_call(functools.partial(kernel, loops, reps, coef, dup), out_sha...]
    unnamed x5 -> x1, local copies, waits for them, and re-layouts: 2.81 us -> 1.77 us
where the time goes in v3:
time: 68.1 us; the launch traced here: 67.9 us
  Pallas kernels  66.1 us (97%)
  local copies, waits for them, and re-layouts  1.77 us (3%)
    pallas_call x1, Pallas kernels, body(): pl.pallas_call(functools.partial(kernel, loops, reps, coef, dup), out_sha...  66.1 us
    unnamed x1, local copies, waits for them, and re-layouts  1.77 us

profile of v3, /device:TPU:0, one launch (start us, length us, event | category | flops | bytes accessed | tf_op | source)
XLA Modules:
  0.0 67.9 jit_solution(12988734746731097517)
XLA Ops:
  0.0 66.1 %shard_map.28 = f32[192,512]{1,0:T(8,128)} custom-call(bf16[192,512]{1,0:T(8,128)(2,1)} %s_hbm.1, bf16[192,2048]{1,0:T(8,128)(2,1)} %t_hbm.1), custom_call_target="tpu_custom_call" | custom-call | flops 2013265920 | bytes 393216 | tf_op jit(solution)/shard_map/pallas_call | solution.py:347
  66.2 1.8 %copy.4 = f32[192,512]{1,0:T(8,128)} copy(f32[192,512]{1,0:T(8,128)} %shard_map.28) | data formatting | bytes 786432

commit v4 on v3

--- a/solution.py
+++ b/solution.py
@@ -11,7 +11,7 @@
 MESH = pl.DeviceIdType.MESH
 LANES = 128
 PIECE = 256
-LAG = 3
+LAG = 6
 EARLY = 2
 IDLE = 4
 EPS = 1e-6
@@ -387,7 +387,7 @@
             dma((2,)),
         ],
         compiler_params=pltpu.CompilerParams(
-            collective_id=0, has_side_effects=True, vmem_limit_bytes=64 * 1024 * 1024
+            collective_id=0, has_side_effects=True, vmem_limit_bytes=65024 * 1024 - 128 * 1024
         ),
         cost_estimate=pl.CostEstimate(flops=flops, bytes_accessed=4 * rows * width, transcendentals=0),
     )(student, teacher)

time: 68.1 us -> 68.8 us (1.010)
  Pallas kernels: 66.1 us -> 66.8 us
    pallas_call x1, Pallas kernels: 66.1 us -> 66.8 us  [body(): pl.pallas_call(functools.partial(kernel, loops, reps, coef, dup), out_sha...]
where the time goes in v4:
time: 68.8 us; the launch traced here: 68.6 us
  Pallas kernels  66.8 us (97%)
  local copies, waits for them, and re-layouts  1.77 us (3%)
    pallas_call x1, Pallas kernels, body(): pl.pallas_call(functools.partial(kernel, loops, reps, coef, dup), out_sha...  66.8 us
    unnamed x1, local copies, waits for them, and re-layouts  1.77 us

profile of v4, /device:TPU:0, one launch (start us, length us, event | category | flops | bytes accessed | tf_op | source)
XLA Modules:
  0.0 68.6 jit_solution(9273788572688142299)
XLA Ops:
  0.0 66.8 %shard_map.28 = f32[192,512]{1,0:T(8,128)} custom-call(bf16[192,512]{1,0:T(8,128)(2,1)} %s_hbm.1, bf16[192,2048]{1,0:T(8,128)(2,1)} %t_hbm.1), custom_call_target="tpu_custom_call" | custom-call | flops 2013265920 | bytes 393216 | tf_op jit(solution)/shard_map/pallas_call | solution.py:347
  66.8 1.8 %copy.4 = f32[192,512]{1,0:T(8,128)} copy(f32[192,512]{1,0:T(8,128)} %shard_map.28) | data formatting | bytes 786432

commit v5 on v2

--- a/solution.py
+++ b/solution.py
@@ -12,15 +12,14 @@
 LANES = 128
 PIECE = 256
 LAG = 3
-EARLY = 2
-IDLE = 4
+IDLE = 6
 EPS = 1e-6
 
 
 def kernel(
     loops, reps, coef, dup, s_hbm, t_hbm, out_ref,
     s_ref, t_ref, stat_tx, stat_rx, inv_keep, cols_all, cols_t, feats, feats_tx, own, right_tx, left_tx,
-    from_left, from_right, full, part_tx, part_rx, part_own, inner_tx, inner_rx,
+    from_left, from_right, acc, part_tx, part_rx, part_own, inner_tx, inner_rx,
     load_sem, stat_sem, strip_send, strip_recv, gather_send, gather_recv, swap_send, swap_recv,
     right_send, right_recv, left_send, left_recv, part_send, part_recv, inner_sem,
 ):
@@ -32,6 +31,8 @@
     t_own = (pieces - 1) // 2
     strips = width // LANES
     steps = strips * pieces
+    early = 2 * strips
+    later = pieces - 2
     sibling = (z, b, 1 - c)
     has_left = z > 0
     has_right = z < loops - 1
@@ -98,22 +99,24 @@
         return remote(feats_tx.at[peer(d), p], feats.at[2 * p, mine],
                       gather_send.at[p, d], gather_recv.at[p, d], (z, peer(d), c))
 
-    for d in range(1, reps):
-        strip_to(d, 0).start()
+    def send_strip(j):
+        if j < strips:
+            for d in range(1, reps):
+                strip_to(d, j).start()
+
+    def send_piece(p):
+        for d in range(1, reps):
+            piece_to(d, p).start()
+
+    send_strip(0)
     for p in range(t_own):
         for q in range(reps):
             lo = (q * t_own + p) * PIECE
             feats_tx[q, p] = (t_ref[:, lo:lo + PIECE].astype(jnp.float32) * inv_t).astype(jnp.bfloat16)
-        for d in range(1, reps):
-            piece_to(d, p).start()
+        if p == 0:
+            send_piece(0)
+            send_strip(1)
         feats[2 * p, mine, :] = feats_tx[b, p]
-    for m in range(strips):
-        for d in range(1, reps):
-            j = lax.rem(peer(d) // dup + m, strips)
-
-            @pl.when(j > 0)
-            def _():
-                strip_to(d, j).start()
 
     block = b // dup
 
@@ -147,10 +150,15 @@
         return remote(part_tx.at[j, peer(d)], part_rx.at[j, d],
                       part_send.at[j, d], part_recv.at[j, d], (z, peer(d), c))
 
+    def strip_and_piece(k):
+        first = k < early
+        j = jnp.where(first, k // 2, (k - early) // later)
+        p = jnp.where(first, lax.rem(k, 2), 2 + lax.rem(k - early + later * strips, later))
+        return j, p
+
     def produce(k):
-        own[k] = jnp.dot(
-            cols_t[k // pieces], feats[lax.rem(k, pieces)], preferred_element_type=jnp.float32
-        )
+        j, p = strip_and_piece(k)
+        own[k] = jnp.dot(cols_t[j], feats[p], preferred_element_type=jnp.float32)
 
     def up(k):
         @pl.when(has_left)
@@ -188,8 +196,7 @@
         return lax.dot_general(left, right, (((1,), (1,)), ((), ())), preferred_element_type=jnp.float32)
 
     def finish(k):
-        j = k // pieces
-        p = lax.rem(k, pieces)
+        j, p = strip_and_piece(k)
 
         @pl.when(has_left)
         def _():
@@ -198,21 +205,26 @@
         @pl.when(has_right)
         def _():
             own[k] = own[k] + from_right[k].astype(jnp.float32)
-        full[p] = own[k].astype(jnp.bfloat16)
-
-        @pl.when(p == pieces - 1)
-        def _():
-            value = across(feats[pieces - 1], full[pieces - 1])
-            if dup > 1:
-                value = value * (1.0 / dup)
-            for q in range(pieces - 1):
-                value = value - across(feats[q], full[q])
+        value = across(feats[p], own[k].astype(jnp.bfloat16))
+        last = p == pieces - 1
+
+        @pl.when(p == 0)
+        def _():
+            acc[j] = value
+
+        @pl.when(jnp.logical_and(p > 0, jnp.logical_not(last)))
+        def _():
+            acc[j] = acc[j] + value
+
+        @pl.when(last)
+        def _():
+            total = value * (1.0 / dup) - acc[j]
             for q in range(reps):
-                part_tx[j, q] = value[q * rows:(q + 1) * rows].astype(jnp.bfloat16)
+                part_tx[j, q] = total[q * rows:(q + 1) * rows].astype(jnp.bfloat16)
 
                 @pl.when(b == q)
                 def _():
-                    part_own[j] = value[q * rows:(q + 1) * rows]
+                    part_own[j] = total[q * rows:(q + 1) * rows]
             for d in range(1, reps):
                 result(j, d).start()
 
@@ -221,8 +233,8 @@
     lag_end = jnp.maximum(lag_up, lag_down)
 
     def chunk_at(i):
-        k = jnp.where(i < EARLY, i, i - IDLE)
-        idle = jnp.logical_and(i >= EARLY, i < EARLY + IDLE)
+        k = jnp.where(i < early, i, i - IDLE)
+        idle = jnp.logical_and(i >= early, i < early + IDLE)
         return k, jnp.logical_and(jnp.logical_not(idle), jnp.logical_and(i >= 0, k < steps))
 
     def tick(i, carry):
@@ -234,46 +246,45 @@
                 act(k)
         return carry
 
-    def made(k):
+    def make(k, carry):
         produce(k)
-        tick(k if k < EARLY else k + IDLE, 0)
+        return tick(jnp.where(k < early, k, k + IDLE), carry)
+
+    def pieces_in(p):
+        for d in range(1, reps):
+            piece_to(d, p).wait_recv()
+            piece_over(d, p).start()
 
     for p in range(t_own):
         piece_over(0, p).start()
     block_over(0).start()
     strip_in(0)
     turn(0)
-    for p in range(t_own):
-        for d in range(1, reps):
-            piece_to(d, p).wait_recv()
-            piece_over(d, p).start()
-        made(2 * p)
-        for d in range(reps):
-            piece_over(d, p).wait_recv()
-        made(2 * p + 1)
-        if p == 0:
-            lax.fori_loop(EARLY, EARLY + IDLE, tick, 0)
-
-    @pl.when(block > 0)
-    def _():
-        strip_in(block)
+    pieces_in(0)
+    send_strip(2)
+    make(0, 0)
+    for d in range(reps):
+        piece_over(d, 0).wait_recv()
+    make(1, 0)
+    for j in range(1, strips):
+        strip_in(j)
+        send_strip(j + 2)
+        if j == min(2, strips - 1):
+            for p in range(1, t_own):
+                send_piece(p)
+        turn(j)
+        lax.fori_loop(2 * j, 2 * j + 2, make, 0)
     for d in range(1, reps):
         block_over(d).start()
     feats[pieces - 1, :, :LANES] = cols_all[:, lanes(block)]
+    lax.fori_loop(early, early + IDLE, tick, 0)
+    for p in range(1, t_own):
+        pieces_in(p)
     for d in range(reps):
+        for p in range(1, t_own):
+            piece_over(d, p).wait_recv()
         block_over(d).wait_recv()
-    made(pieces - 1)
-    for j in range(1, strips):
-        @pl.when(block != j)
-        def _():
-            strip_in(j)
-        turn(j)
-
-        def make(k, carry):
-            produce(k)
-            return tick(k + IDLE, carry)
-
-        lax.fori_loop(j * pieces, (j + 1) * pieces, make, 0)
+    lax.fori_loop(early, steps, make, 0)
     lax.fori_loop(steps + IDLE, steps + IDLE + LAG * (loops - 1), tick, 0)
 
     norm = cols_all[mine, :].astype(jnp.float32)
@@ -354,7 +365,7 @@
             pltpu.VMEM((steps, LANES, PIECE), bf16),
             pltpu.VMEM((steps, LANES, PIECE), bf16),
             pltpu.VMEM((steps, LANES, PIECE), bf16),
-            pltpu.VMEM((pieces, LANES, PIECE), bf16),
+            pltpu.VMEM((strips, total, LANES), f32),
             pltpu.VMEM((strips, reps, rows, LANES), bf16),
             pltpu.VMEM((strips, reps, rows, LANES), bf16),
             pltpu.VMEM((strips, rows, LANES), f32),

time: 67 us -> 71.4 us (1.066)
  Pallas kernels: 64 us -> 68.4 us
    pallas_call x1, Pallas kernels: 64 us -> 68.4 us  [body(): pl.pallas_call(functools.partial(kernel, loops, reps, coef, dup), out_sha...]
where the time goes in v5:
time: 71.4 us; the launch traced here: 71.2 us
  Pallas kernels  68.4 us (96%)
  local copies, waits for them, and re-layouts  2.81 us (4%)
    pallas_call x1, Pallas kernels, body(): pl.pallas_call(functools.partial(kernel, loops, reps, coef, dup), out_sha...  68.4 us
    unnamed x5, local copies, waits for them, and re-layouts  2.81 us

profile of v5, /device:TPU:0, one launch (start us, length us, event | category | flops | bytes accessed | tf_op | source)
XLA Modules:
  0.0 71.2 jit_solution(15708322924099401587)
XLA Ops:
  0.0 0.0 copy-start
  0.0 1.1 %copy-done = bf16[192,2048]{1,0:T(8,128)(2,1)S(1)} copy-done((bf16[192,2048]{1,0:T(8,128)(2,1)S(1)}, bf16[192,2048]{1,0:T(8,128)(2,1)}, u32[]{:S(2)}) %copy-start) | copy-done | bytes 786456
  1.1 0.0 copy-start.1
  1.1 0.9 %copy-done.1 = bf16[192,512]{1,0:T(8,128)(2,1)S(1)} copy-done((bf16[192,512]{1,0:T(8,128)(2,1)S(1)}, bf16[192,512]{1,0:T(8,128)(2,1)}, u32[]{:S(2)}) %copy-start.1) | copy-done | bytes 196632
  2.1 68.4 %shard_map.28 = f32[192,512]{1,0:T(8,128)S(1)} custom-call(bf16[192,512]{1,0:T(8,128)(2,1)S(1)} %copy-done.1, bf16[192,2048]{1,0:T(8,128)(2,1)S(1)} %copy-done), custom_call_target="tpu_custom_call" | custom-call | flops 2013265920 | bytes 393216 | tf_op jit(solution)/shard_map/pallas_call | solution.py:348
  70.4 0.7 %copy.4 = f32[192,512]{1,0:T(8,128)} copy(f32[192,512]{1,0:T(8,128)S(1)} %shard_map.28) | data formatting | bytes 786432
Async XLA Ops:
  0.0 1.1 %copy-start = (bf16[192,2048]{1,0:T(8,128)(2,1)S(1)}, bf16[192,2048]{1,0:T(8,128)(2,1)}, u32[]{:S(2)}) copy-start(bf16[192,2048]{1,0:T(8,128)(2,1)} %t_hbm.1) | copy-start | bytes 2359300
  1.1 0.9 %copy-start.1 = (bf16[192,512]{1,0:T(8,128)(2,1)S(1)}, bf16[192,512]{1,0:T(8,128)(2,1)}, u32[]{:S(2)}) copy-start(bf16[192,512]{1,0:T(8,128)(2,1)} %s_hbm.1) | copy-start | bytes 589828

commit v6 on v2

--- a/solution.py
+++ b/solution.py
@@ -11,8 +11,9 @@
 MESH = pl.DeviceIdType.MESH
 LANES = 128
 PIECE = 256
+STRIP = 256
+HALF = 128
 LAG = 3
-EARLY = 2
 IDLE = 4
 EPS = 1e-6
 
@@ -20,7 +21,7 @@
 def kernel(
     loops, reps, coef, dup, s_hbm, t_hbm, out_ref,
     s_ref, t_ref, stat_tx, stat_rx, inv_keep, cols_all, cols_t, feats, feats_tx, own, right_tx, left_tx,
-    from_left, from_right, full, part_tx, part_rx, part_own, inner_tx, inner_rx,
+    from_left, from_right, acc, part_tx, part_rx, part_own, inner_tx, inner_rx, whole,
     load_sem, stat_sem, strip_send, strip_recv, gather_send, gather_recv, swap_send, swap_recv,
     right_send, right_recv, left_send, left_recv, part_send, part_recv, inner_sem,
 ):
@@ -30,8 +31,9 @@
     rows, width = s_ref.shape
     pieces, total_rows, _ = feats.shape
     t_own = (pieces - 1) // 2
-    strips = width // LANES
+    strips = width // STRIP
     steps = strips * pieces
+    ticks = 2 * steps
     sibling = (z, b, 1 - c)
     has_left = z > 0
     has_right = z < loops - 1
@@ -90,7 +92,7 @@
     cols_all[mine, :] = (s_ref[...].astype(jnp.float32) * inv_s).astype(jnp.bfloat16)
 
     def strip_to(d, j):
-        at = lanes(j)
+        at = slice(j * STRIP, (j + 1) * STRIP)
         return remote(cols_all.at[mine, at], cols_all.at[mine, at],
                       strip_send.at[j, d], strip_recv.at[j, d], (z, peer(d), c))
 
@@ -107,13 +109,9 @@
         for d in range(1, reps):
             piece_to(d, p).start()
         feats[2 * p, mine, :] = feats_tx[b, p]
-    for m in range(strips):
-        for d in range(1, reps):
-            j = lax.rem(peer(d) // dup + m, strips)
-
-            @pl.when(j > 0)
-            def _():
-                strip_to(d, j).start()
+    for j in range(1, strips):
+        for d in range(1, reps):
+            strip_to(d, j).start()
 
     block = b // dup
 
@@ -135,7 +133,7 @@
             strip_to(d, j).wait_recv()
 
     def turn(j):
-        cols_t[j] = cols_all[:, j * LANES:(j + 1) * LANES].T
+        cols_t[j] = cols_all[:, j * STRIP:(j + 1) * STRIP].T
 
     def rightward(k):
         return remote(right_tx.at[k], from_left.at[k], right_send.at[k], right_recv.at[k], (z + 1, b, c))
@@ -148,9 +146,11 @@
                       part_send.at[j, d], part_recv.at[j, d], (z, peer(d), c))
 
     def produce(k):
-        own[k] = jnp.dot(
+        value = jnp.dot(
             cols_t[k // pieces], feats[lax.rem(k, pieces)], preferred_element_type=jnp.float32
         )
+        own[2 * k] = value[:HALF]
+        own[2 * k + 1] = value[HALF:]
 
     def up(k):
         @pl.when(has_left)
@@ -190,53 +190,73 @@
     def finish(k):
         j = k // pieces
         p = lax.rem(k, pieces)
-
-        @pl.when(has_left)
-        def _():
-            own[k] = own[k] + from_left[k].astype(jnp.float32)
-
-        @pl.when(has_right)
-        def _():
-            own[k] = own[k] + from_right[k].astype(jnp.float32)
-        full[p] = own[k].astype(jnp.bfloat16)
-
-        @pl.when(p == pieces - 1)
-        def _():
-            value = across(feats[pieces - 1], full[pieces - 1])
-            if dup > 1:
-                value = value * (1.0 / dup)
-            for q in range(pieces - 1):
-                value = value - across(feats[q], full[q])
+        both = pl.ds(2 * k, 2)
+
+        def joined(ref):
+            return ref[both].reshape(STRIP, PIECE).astype(jnp.float32)
+
+        @pl.when(jnp.logical_and(has_left, has_right))
+        def _():
+            whole[...] = (joined(own) + joined(from_left) + joined(from_right)).astype(jnp.bfloat16)
+
+        @pl.when(jnp.logical_not(has_left))
+        def _():
+            whole[...] = (joined(own) + joined(from_right)).astype(jnp.bfloat16)
+
+        @pl.when(jnp.logical_not(has_right))
+        def _():
+            whole[...] = (joined(own) + joined(from_left)).astype(jnp.bfloat16)
+        value = across(feats[p], whole[...])
+        last = p == pieces - 1
+
+        @pl.when(p == 0)
+        def _():
+            acc[...] = value
+
+        @pl.when(jnp.logical_and(p > 0, jnp.logical_not(last)))
+        def _():
+            acc[...] = acc[...] + value
+
+        @pl.when(last)
+        def _():
+            total = value * (1.0 / dup) - acc[...]
             for q in range(reps):
-                part_tx[j, q] = value[q * rows:(q + 1) * rows].astype(jnp.bfloat16)
+                part_tx[j, q] = total[q * rows:(q + 1) * rows].astype(jnp.bfloat16)
 
                 @pl.when(b == q)
                 def _():
-                    part_own[j] = value[q * rows:(q + 1) * rows]
+                    part_own[j] = total[q * rows:(q + 1) * rows]
             for d in range(1, reps):
                 result(j, d).start()
 
     lag_up = LAG * z
     lag_down = LAG * (loops - 1 - z)
     lag_end = jnp.maximum(lag_up, lag_down)
-
-    def chunk_at(i):
-        k = jnp.where(i < EARLY, i, i - IDLE)
-        idle = jnp.logical_and(i >= EARLY, i < EARLY + IDLE)
-        return k, jnp.logical_and(jnp.logical_not(idle), jnp.logical_and(i >= 0, k < steps))
+    early = 4
+
+    def half_at(i):
+        h = jnp.where(i < early, i, i - IDLE)
+        idle = jnp.logical_and(i >= early, i < early + IDLE)
+        return h, jnp.logical_and(jnp.logical_not(idle), jnp.logical_and(i >= 0, h < ticks))
 
     def tick(i, carry):
-        for lag, act in ((lag_up, up), (lag_down, down), (lag_end, finish)):
-            k, live = chunk_at(i - lag)
+        for lag, act in ((lag_up, up), (lag_down, down)):
+            h, live = half_at(i - lag)
 
             @pl.when(live)
             def _():
-                act(k)
+                act(h)
+        h, live = half_at(i - lag_end)
+
+        @pl.when(jnp.logical_and(live, lax.rem(h, 2) == 1))
+        def _():
+            finish(h // 2)
         return carry
 
-    def made(k):
+    def make(k, carry):
         produce(k)
-        tick(k if k < EARLY else k + IDLE, 0)
+        first = 2 * k if isinstance(k, int) and k < 2 else 2 * k + IDLE
+        return lax.fori_loop(first, first + 2, tick, carry)
 
     for p in range(t_own):
         piece_over(0, p).start()
@@ -247,34 +267,23 @@
         for d in range(1, reps):
             piece_to(d, p).wait_recv()
             piece_over(d, p).start()
-        made(2 * p)
+        make(2 * p, 0)
         for d in range(reps):
             piece_over(d, p).wait_recv()
-        made(2 * p + 1)
+        make(2 * p + 1, 0)
         if p == 0:
-            lax.fori_loop(EARLY, EARLY + IDLE, tick, 0)
-
-    @pl.when(block > 0)
-    def _():
-        strip_in(block)
+            lax.fori_loop(early, early + IDLE, tick, 0)
+    for j in range(1, strips):
+        strip_in(j)
     for d in range(1, reps):
         block_over(d).start()
     feats[pieces - 1, :, :LANES] = cols_all[:, lanes(block)]
+    for j in range(1, strips):
+        turn(j)
     for d in range(reps):
         block_over(d).wait_recv()
-    made(pieces - 1)
-    for j in range(1, strips):
-        @pl.when(block != j)
-        def _():
-            strip_in(j)
-        turn(j)
-
-        def make(k, carry):
-            produce(k)
-            return tick(k + IDLE, carry)
-
-        lax.fori_loop(j * pieces, (j + 1) * pieces, make, 0)
-    lax.fori_loop(steps + IDLE, steps + IDLE + LAG * (loops - 1), tick, 0)
+    lax.fori_loop(pieces - 1, steps, make, 0)
+    lax.fori_loop(ticks + IDLE, ticks + IDLE + LAG * (loops - 1), tick, 0)
 
     norm = cols_all[mine, :].astype(jnp.float32)
     inner = jnp.zeros((rows, 1), jnp.float32)
@@ -286,15 +295,16 @@
             grad = grad + part_rx[j, d].astype(jnp.float32)
         grad = grad * coef
         grads.append(grad)
-        inner = inner + jnp.sum(grad * norm[:, j * LANES:(j + 1) * LANES], axis=1, keepdims=True)
+        inner = inner + jnp.sum(grad * norm[:, j * STRIP:(j + 1) * STRIP], axis=1, keepdims=True)
     inner_tx[...] = jnp.broadcast_to(inner, (rows, LANES))
     swap = remote(inner_tx, inner_rx, inner_sem.at[0], inner_sem.at[1], sibling)
     swap.start()
     swap.wait_recv()
-    inner_all = inner_tx[...] + inner_rx[...]
+    inner_all = (inner_tx[...] + inner_rx[...])[:, :1]
+    scale = inv_keep[...][:, :1]
     for j in range(strips):
-        at = slice(j * LANES, (j + 1) * LANES)
-        out_ref[:, at] = (grads[j] - inner_all * norm[:, at]) * inv_keep[...]
+        at = slice(j * STRIP, (j + 1) * STRIP)
+        out_ref[:, at] = (grads[j] - inner_all * norm[:, at]) * scale
 
     swap.wait_send()
     for d in range(reps):
@@ -318,7 +328,7 @@
             leftward(k).wait_send()
         return carry
 
-    lax.fori_loop(0, steps, drain, 0)
+    lax.fori_loop(0, ticks, drain, 0)
 
 
 def body(loops, reps, student, teacher):
@@ -328,8 +338,8 @@
     dup = max(1, reps * LANES // width)
     t_own = teacher.shape[1] // (reps * PIECE)
     pieces = 1 + 2 * t_own
-    strips = width // LANES
-    steps = strips * pieces
+    strips = width // STRIP
+    ticks = 2 * strips * pieces
     total = rows * reps
     f32, bf16 = jnp.float32, jnp.bfloat16
     dma = pltpu.SemaphoreType.DMA
@@ -346,20 +356,21 @@
             pltpu.VMEM((rows, LANES), f32),
             pltpu.VMEM((rows, LANES), f32),
             pltpu.VMEM((total, width), bf16),
-            pltpu.VMEM((strips, LANES, total), bf16),
+            pltpu.VMEM((strips, STRIP, total), bf16),
             pltpu.VMEM((pieces, total, PIECE), bf16),
             pltpu.VMEM((reps, t_own, rows, PIECE), bf16),
-            pltpu.VMEM((steps, LANES, PIECE), f32),
-            pltpu.VMEM((steps, LANES, PIECE), bf16),
-            pltpu.VMEM((steps, LANES, PIECE), bf16),
-            pltpu.VMEM((steps, LANES, PIECE), bf16),
-            pltpu.VMEM((steps, LANES, PIECE), bf16),
-            pltpu.VMEM((pieces, LANES, PIECE), bf16),
-            pltpu.VMEM((strips, reps, rows, LANES), bf16),
-            pltpu.VMEM((strips, reps, rows, LANES), bf16),
-            pltpu.VMEM((strips, rows, LANES), f32),
+            pltpu.VMEM((ticks, HALF, PIECE), f32),
+            pltpu.VMEM((ticks, HALF, PIECE), bf16),
+            pltpu.VMEM((ticks, HALF, PIECE), bf16),
+            pltpu.VMEM((ticks, HALF, PIECE), bf16),
+            pltpu.VMEM((ticks, HALF, PIECE), bf16),
+            pltpu.VMEM((total, STRIP), f32),
+            pltpu.VMEM((strips, reps, rows, STRIP), bf16),
+            pltpu.VMEM((strips, reps, rows, STRIP), bf16),
+            pltpu.VMEM((strips, rows, STRIP), f32),
             pltpu.VMEM((rows, LANES), f32),
             pltpu.VMEM((rows, LANES), f32),
+            pltpu.VMEM((STRIP, PIECE), bf16),
             dma((2,)),
             dma((2,)),
             dma((strips, reps)),
@@ -368,10 +379,10 @@
             dma((t_own, reps)),
             dma((t_own + 1, reps)),
             dma((t_own + 1, reps)),
-            dma((steps,)),
-            dma((steps,)),
-            dma((steps,)),
-            dma((steps,)),
+            dma((ticks,)),
+            dma((ticks,)),
+            dma((ticks,)),
+            dma((ticks,)),
             dma((strips, reps)),
             dma((strips, reps)),
             dma((2,)),

time: 67 us -> 71.9 us (1.073)
  Pallas kernels: 64 us -> 68.9 us
    pallas_call x1, Pallas kernels: 64 us -> 68.9 us  [body(): pl.pallas_call(functools.partial(kernel, loops, reps, coef, dup), out_sha...]
where the time goes in v6:
time: 71.9 us; the launch traced here: 71.7 us
  Pallas kernels  68.9 us (96%)
  local copies, waits for them, and re-layouts  2.81 us (4%)
    pallas_call x1, Pallas kernels, body(): pl.pallas_call(functools.partial(kernel, loops, reps, coef, dup), out_sha...  68.9 us
    unnamed x5, local copies, waits for them, and re-layouts  2.81 us

profile of v6, /device:TPU:0, one launch (start us, length us, event | category | flops | bytes accessed | tf_op | source)
XLA Modules:
  0.0 71.7 jit_solution(550642689215919857)
XLA Ops:
  0.0 0.0 copy-start
  0.0 1.1 %copy-done = bf16[192,2048]{1,0:T(8,128)(2,1)S(1)} copy-done((bf16[192,2048]{1,0:T(8,128)(2,1)S(1)}, bf16[192,2048]{1,0:T(8,128)(2,1)}, u32[]{:S(2)}) %copy-start) | copy-done | bytes 786456
  1.1 0.0 copy-start.1
  1.1 0.9 %copy-done.1 = bf16[192,512]{1,0:T(8,128)(2,1)S(1)} copy-done((bf16[192,512]{1,0:T(8,128)(2,1)S(1)}, bf16[192,512]{1,0:T(8,128)(2,1)}, u32[]{:S(2)}) %copy-start.1) | copy-done | bytes 196632
  2.1 68.9 %shard_map.28 = f32[192,512]{1,0:T(8,128)S(1)} custom-call(bf16[192,512]{1,0:T(8,128)(2,1)S(1)} %copy-done.1, bf16[192,2048]{1,0:T(8,128)(2,1)S(1)} %copy-done), custom_call_target="tpu_custom_call" | custom-call | flops 2013265920 | bytes 393216 | tf_op jit(solution)/shard_map/pallas_call | solution.py:347
  70.9 0.7 %copy.4 = f32[192,512]{1,0:T(8,128)} copy(f32[192,512]{1,0:T(8,128)S(1)} %shard_map.28) | data formatting | bytes 786432
Async XLA Ops:
  0.0 1.1 %copy-start = (bf16[192,2048]{1,0:T(8,128)(2,1)S(1)}, bf16[192,2048]{1,0:T(8,128)(2,1)}, u32[]{:S(2)}) copy-start(bf16[192,2048]{1,0:T(8,128)(2,1)} %t_hbm.1) | copy-start | bytes 2359300
  1.1 0.9 %copy-start.1 = (bf16[192,512]{1,0:T(8,128)(2,1)S(1)}, bf16[192,512]{1,0:T(8,128)(2,1)}, u32[]{:S(2)}) copy-start(bf16[192,512]{1,0:T(8,128)(2,1)} %s_hbm.1) | copy-start | bytes 589828

commit v7 on v5

--- a/solution.py
+++ b/solution.py
@@ -12,14 +12,14 @@
 LANES = 128
 PIECE = 256
 LAG = 3
-IDLE = 6
+IDLE = 3
 EPS = 1e-6
 
 
 def kernel(
     loops, reps, coef, dup, s_hbm, t_hbm, out_ref,
     s_ref, t_ref, stat_tx, stat_rx, inv_keep, cols_all, cols_t, feats, feats_tx, own, right_tx, left_tx,
-    from_left, from_right, acc, part_tx, part_rx, part_own, inner_tx, inner_rx,
+    from_left, from_right, full, part_tx, part_rx, part_own, inner_tx, inner_rx,
     load_sem, stat_sem, strip_send, strip_recv, gather_send, gather_recv, swap_send, swap_recv,
     right_send, right_recv, left_send, left_recv, part_send, part_recv, inner_sem,
 ):
@@ -198,27 +198,28 @@
     def finish(k):
         j, p = strip_and_piece(k)
 
-        @pl.when(has_left)
-        def _():
-            own[k] = own[k] + from_left[k].astype(jnp.float32)
-
-        @pl.when(has_right)
-        def _():
-            own[k] = own[k] + from_right[k].astype(jnp.float32)
-        value = across(feats[p], own[k].astype(jnp.bfloat16))
         last = p == pieces - 1
-
-        @pl.when(p == 0)
-        def _():
-            acc[j] = value
-
-        @pl.when(jnp.logical_and(p > 0, jnp.logical_not(last)))
-        def _():
-            acc[j] = acc[j] + value
+        sign = jnp.where(last, 1.0 / dup, -1.0)
+
+        @pl.when(jnp.logical_and(has_left, has_right))
+        def _():
+            total = own[k] + from_left[k].astype(jnp.float32) + from_right[k].astype(jnp.float32)
+            full[j, p] = (total * sign).astype(jnp.bfloat16)
+
+        @pl.when(jnp.logical_not(has_left))
+        def _():
+            full[j, p] = ((own[k] + from_right[k].astype(jnp.float32)) * sign).astype(jnp.bfloat16)
+
+        @pl.when(jnp.logical_not(has_right))
+        def _():
+            full[j, p] = ((own[k] + from_left[k].astype(jnp.float32)) * sign).astype(jnp.bfloat16)
 
         @pl.when(last)
         def _():
-            total = value * (1.0 / dup) - acc[j]
+            total = across(
+                jnp.concatenate([feats[q] for q in range(pieces)], axis=1),
+                jnp.concatenate([full[j, q] for q in range(pieces)], axis=1),
+            )
             for q in range(reps):
                 part_tx[j, q] = total[q * rows:(q + 1) * rows].astype(jnp.bfloat16)
 
@@ -365,7 +366,7 @@
             pltpu.VMEM((steps, LANES, PIECE), bf16),
             pltpu.VMEM((steps, LANES, PIECE), bf16),
             pltpu.VMEM((steps, LANES, PIECE), bf16),
-            pltpu.VMEM((strips, total, LANES), f32),
+            pltpu.VMEM((strips, pieces, LANES, PIECE), bf16),
             pltpu.VMEM((strips, reps, rows, LANES), bf16),
             pltpu.VMEM((strips, reps, rows, LANES), bf16),
             pltpu.VMEM((strips, rows, LANES), f32),

time: 71.4 us -> 67.2 us (0.941)
  Pallas kernels: 68.4 us -> 64.2 us
    pallas_call x1, Pallas kernels: 68.4 us -> 64.2 us  [body(): pl.pallas_call(functools.partial(kernel, loops, reps, coef, dup), out_sha...]
where the time goes in v7:
time: 67.2 us; the launch traced here: 67 us
  Pallas kernels  64.2 us (96%)
  local copies, waits for them, and re-layouts  2.81 us (4%)
    pallas_call x1, Pallas kernels, body(): pl.pallas_call(functools.partial(kernel, loops, reps, coef, dup), out_sha...  64.2 us
    unnamed x5, local copies, waits for them, and re-layouts  2.81 us

profile of v7, /device:TPU:0, one launch (start us, length us, event | category | flops | bytes accessed | tf_op | source)
XLA Modules:
  0.0 67.0 jit_solution(16696523869032874912)
XLA Ops:
  0.0 0.0 copy-start
  0.0 1.1 %copy-done = bf16[192,2048]{1,0:T(8,128)(2,1)S(1)} copy-done((bf16[192,2048]{1,0:T(8,128)(2,1)S(1)}, bf16[192,2048]{1,0:T(8,128)(2,1)}, u32[]{:S(2)}) %copy-start) | copy-done | bytes 786456
  1.1 0.0 copy-start.1
  1.1 0.9 %copy-done.1 = bf16[192,512]{1,0:T(8,128)(2,1)S(1)} copy-done((bf16[192,512]{1,0:T(8,128)(2,1)S(1)}, bf16[192,512]{1,0:T(8,128)(2,1)}, u32[]{:S(2)}) %copy-start.1) | copy-done | bytes 196632
  2.1 64.2 %shard_map.28 = f32[192,512]{1,0:T(8,128)S(1)} custom-call(bf16[192,512]{1,0:T(8,128)(2,1)S(1)} %copy-done.1, bf16[192,2048]{1,0:T(8,128)(2,1)S(1)} %copy-done), custom_call_target="tpu_custom_call" | custom-call | flops 2013265920 | bytes 393216 | tf_op jit(solution)/shard_map/pallas_call | solution.py:349
  66.2 0.7 %copy.4 = f32[192,512]{1,0:T(8,128)} copy(f32[192,512]{1,0:T(8,128)S(1)} %shard_map.28) | data formatting | bytes 786432
Async XLA Ops:
  0.0 1.1 %copy-start = (bf16[192,2048]{1,0:T(8,128)(2,1)S(1)}, bf16[192,2048]{1,0:T(8,128)(2,1)}, u32[]{:S(2)}) copy-start(bf16[192,2048]{1,0:T(8,128)(2,1)} %t_hbm.1) | copy-start | bytes 2359300
  1.1 0.9 %copy-start.1 = (bf16[192,512]{1,0:T(8,128)(2,1)S(1)}, bf16[192,512]{1,0:T(8,128)(2,1)}, u32[]{:S(2)}) copy-start(bf16[192,512]{1,0:T(8,128)(2,1)} %s_hbm.1) | copy-start | bytes 589828

commit v8 on v7

--- a/solution.py
+++ b/solution.py
@@ -11,8 +11,8 @@
 MESH = pl.DeviceIdType.MESH
 LANES = 128
 PIECE = 256
-LAG = 3
-IDLE = 3
+LAG = 2
+IDLE = 2
 EPS = 1e-6
 
 
@@ -302,13 +302,6 @@
     inner_tx[...] = jnp.broadcast_to(inner, (rows, LANES))
     swap = remote(inner_tx, inner_rx, inner_sem.at[0], inner_sem.at[1], sibling)
     swap.start()
-    swap.wait_recv()
-    inner_all = inner_tx[...] + inner_rx[...]
-    for j in range(strips):
-        at = slice(j * LANES, (j + 1) * LANES)
-        out_ref[:, at] = (grads[j] - inner_all * norm[:, at]) * inv_keep[...]
-
-    swap.wait_send()
     for d in range(reps):
         for p in range(t_own):
             piece_over(d, p).wait_send()
@@ -331,6 +324,14 @@
         return carry
 
     lax.fori_loop(0, steps, drain, 0)
+
+    swap.wait_recv()
+    inner_all = inner_tx[...] + inner_rx[...]
+    for j in range(strips):
+        at = slice(j * LANES, (j + 1) * LANES)
+        out_ref[:, at] = (grads[j] - inner_all * norm[:, at]) * inv_keep[...]
+
+    swap.wait_send()
 
 
 def body(loops, reps, student, teacher):

time: 67.2 us -> 71.7 us (1.067)
  Pallas kernels: 64.2 us -> 68.7 us
    pallas_call x1, Pallas kernels: 64.2 us -> 68.7 us  [body(): pl.pallas_call(functools.partial(kernel, loops, reps, coef, dup), out_sha...]
where the time goes in v8:
time: 71.7 us; the launch traced here: 71.5 us
  Pallas kernels  68.7 us (96%)
  local copies, waits for them, and re-layouts  2.81 us (4%)
    pallas_call x1, Pallas kernels, body(): pl.pallas_call(functools.partial(kernel, loops, reps, coef, dup), out_sha...  68.7 us
    unnamed x5, local copies, waits for them, and re-layouts  2.81 us

profile of v8, /device:TPU:0, one launch (start us, length us, event | category | flops | bytes accessed | tf_op | source)
XLA Modules:
  0.0 71.5 jit_solution(1719697626400107725)
XLA Ops:
  0.0 0.0 copy-start
  0.0 1.1 %copy-done = bf16[192,2048]{1,0:T(8,128)(2,1)S(1)} copy-done((bf16[192,2048]{1,0:T(8,128)(2,1)S(1)}, bf16[192,2048]{1,0:T(8,128)(2,1)}, u32[]{:S(2)}) %copy-start) | copy-done | bytes 786456
  1.1 0.0 copy-start.1
  1.1 0.9 %copy-done.1 = bf16[192,512]{1,0:T(8,128)(2,1)S(1)} copy-done((bf16[192,512]{1,0:T(8,128)(2,1)S(1)}, bf16[192,512]{1,0:T(8,128)(2,1)}, u32[]{:S(2)}) %copy-start.1) | copy-done | bytes 196632
  2.1 68.7 %shard_map.28 = f32[192,512]{1,0:T(8,128)S(1)} custom-call(bf16[192,512]{1,0:T(8,128)(2,1)S(1)} %copy-done.1, bf16[192,2048]{1,0:T(8,128)(2,1)S(1)} %copy-done), custom_call_target="tpu_custom_call" | custom-call | flops 2013265920 | bytes 393216 | tf_op jit(solution)/shard_map/pallas_call | solution.py:350
  70.8 0.7 %copy.4 = f32[192,512]{1,0:T(8,128)} copy(f32[192,512]{1,0:T(8,128)S(1)} %shard_map.28) | data formatting | bytes 786432
Async XLA Ops:
  0.0 1.1 %copy-start = (bf16[192,2048]{1,0:T(8,128)(2,1)S(1)}, bf16[192,2048]{1,0:T(8,128)(2,1)}, u32[]{:S(2)}) copy-start(bf16[192,2048]{1,0:T(8,128)(2,1)} %t_hbm.1) | copy-start | bytes 2359300
  1.1 0.9 %copy-start.1 = (bf16[192,512]{1,0:T(8,128)(2,1)S(1)}, bf16[192,512]{1,0:T(8,128)(2,1)}, u32[]{:S(2)}) copy-start(bf16[192,512]{1,0:T(8,128)(2,1)} %s_hbm.1) | copy-start | bytes 589828

commit v9 on v8

--- a/solution.py
+++ b/solution.py
@@ -11,8 +11,8 @@
 MESH = pl.DeviceIdType.MESH
 LANES = 128
 PIECE = 256
-LAG = 2
-IDLE = 2
+LAG = 3
+IDLE = 3
 EPS = 1e-6
 
 
@@ -239,12 +239,18 @@
         return k, jnp.logical_and(jnp.logical_not(idle), jnp.logical_and(i >= 0, k < steps))
 
     def tick(i, carry):
-        for lag, act in ((lag_up, up), (lag_down, down), (lag_end, finish)):
+        def serve(lag, act, when=True):
             k, live = chunk_at(i - lag)
 
-            @pl.when(live)
+            @pl.when(jnp.logical_and(live, when))
             def _():
                 act(k)
+
+        lower = lag_down > lag_up
+        serve(lag_down, down, lower)
+        serve(lag_up, up)
+        serve(lag_down, down, jnp.logical_not(lower))
+        serve(lag_end, finish)
         return carry
 
     def make(k, carry):

time: 71.7 us -> 66.6 us (0.929)
  Pallas kernels: 68.7 us -> 63.6 us
    pallas_call x1, Pallas kernels: 68.7 us -> 63.6 us  [body(): pl.pallas_call(functools.partial(kernel, loops, reps, coef, dup), out_sha...]
where the time goes in v9:
time: 66.6 us; the launch traced here: 66.4 us
  Pallas kernels  63.6 us (95%)
  local copies, waits for them, and re-layouts  2.81 us (4%)
    pallas_call x1, Pallas kernels, body(): pl.pallas_call(functools.partial(kernel, loops, reps, coef, dup), out_sha...  63.6 us
    unnamed x5, local copies, waits for them, and re-layouts  2.81 us

profile of v9, /device:TPU:0, one launch (start us, length us, event | category | flops | bytes accessed | tf_op | source)
XLA Modules:
  0.0 66.4 jit_solution(18284930533923926660)
XLA Ops:
  0.0 0.0 copy-start
  0.0 1.1 %copy-done = bf16[192,2048]{1,0:T(8,128)(2,1)S(1)} copy-done((bf16[192,2048]{1,0:T(8,128)(2,1)S(1)}, bf16[192,2048]{1,0:T(8,128)(2,1)}, u32[]{:S(2)}) %copy-start) | copy-done | bytes 786456
  1.1 0.0 copy-start.1
  1.1 0.9 %copy-done.1 = bf16[192,512]{1,0:T(8,128)(2,1)S(1)} copy-done((bf16[192,512]{1,0:T(8,128)(2,1)S(1)}, bf16[192,512]{1,0:T(8,128)(2,1)}, u32[]{:S(2)}) %copy-start.1) | copy-done | bytes 196632
  2.1 63.6 %shard_map.28 = f32[192,512]{1,0:T(8,128)S(1)} custom-call(bf16[192,512]{1,0:T(8,128)(2,1)S(1)} %copy-done.1, bf16[192,2048]{1,0:T(8,128)(2,1)S(1)} %copy-done), custom_call_target="tpu_custom_call" | custom-call | flops 2013265920 | bytes 393216 | tf_op jit(solution)/shard_map/pallas_call | solution.py:356
  65.7 0.7 %copy.4 = f32[192,512]{1,0:T(8,128)} copy(f32[192,512]{1,0:T(8,128)S(1)} %shard_map.28) | data formatting | bytes 786432
Async XLA Ops:
  0.0 1.1 %copy-start = (bf16[192,2048]{1,0:T(8,128)(2,1)S(1)}, bf16[192,2048]{1,0:T(8,128)(2,1)}, u32[]{:S(2)}) copy-start(bf16[192,2048]{1,0:T(8,128)(2,1)} %t_hbm.1) | copy-start | bytes 2359300
  1.1 0.9 %copy-start.1 = (bf16[192,512]{1,0:T(8,128)(2,1)S(1)}, bf16[192,512]{1,0:T(8,128)(2,1)}, u32[]{:S(2)}) copy-start(bf16[192,512]{1,0:T(8,128)(2,1)} %s_hbm.1) | copy-start | bytes 589828

commit v10 on v9

--- a/solution.py
+++ b/solution.py
@@ -268,15 +268,15 @@
     strip_in(0)
     turn(0)
     pieces_in(0)
-    send_strip(2)
+    for j in range(2, strips):
+        send_strip(j)
     make(0, 0)
     for d in range(reps):
         piece_over(d, 0).wait_recv()
     make(1, 0)
     for j in range(1, strips):
         strip_in(j)
-        send_strip(j + 2)
-        if j == min(2, strips - 1):
+        if j == 1:
             for p in range(1, t_own):
                 send_piece(p)
         turn(j)

time: 66.6 us -> 66.6 us (level)
  no operation moved by 1% of the time
where the time goes in v10:
time: 66.6 us; the launch traced here: 66.4 us
  Pallas kernels  63.6 us (95%)
  local copies, waits for them, and re-layouts  2.81 us (4%)
    pallas_call x1, Pallas kernels, body(): pl.pallas_call(functools.partial(kernel, loops, reps, coef, dup), out_sha...  63.6 us
    unnamed x5, local copies, waits for them, and re-layouts  2.81 us

profile of v10, /device:TPU:0, one launch (start us, length us, event | category | flops | bytes accessed | tf_op | source)
XLA Modules:
  0.0 66.4 jit_solution(9243097180784242314)
XLA Ops:
  0.0 0.0 copy-start
  0.0 1.1 %copy-done = bf16[192,2048]{1,0:T(8,128)(2,1)S(1)} copy-done((bf16[192,2048]{1,0:T(8,128)(2,1)S(1)}, bf16[192,2048]{1,0:T(8,128)(2,1)}, u32[]{:S(2)}) %copy-start) | copy-done | bytes 786456
  1.1 0.0 copy-start.1
  1.1 0.9 %copy-done.1 = bf16[192,512]{1,0:T(8,128)(2,1)S(1)} copy-done((bf16[192,512]{1,0:T(8,128)(2,1)S(1)}, bf16[192,512]{1,0:T(8,128)(2,1)}, u32[]{:S(2)}) %copy-start.1) | copy-done | bytes 196632
  2.1 63.6 %shard_map.28 = f32[192,512]{1,0:T(8,128)S(1)} custom-call(bf16[192,512]{1,0:T(8,128)(2,1)S(1)} %copy-done.1, bf16[192,2048]{1,0:T(8,128)(2,1)S(1)} %copy-done), custom_call_target="tpu_custom_call" | custom-call | flops 2013265920 | bytes 393216 | tf_op jit(solution)/shard_map/pallas_call | solution.py:356
  65.7 0.7 %copy.4 = f32[192,512]{1,0:T(8,128)} copy(f32[192,512]{1,0:T(8,128)S(1)} %shard_map.28) | data formatting | bytes 786432
Async XLA Ops:
  0.0 1.1 %copy-start = (bf16[192,2048]{1,0:T(8,128)(2,1)S(1)}, bf16[192,2048]{1,0:T(8,128)(2,1)}, u32[]{:S(2)}) copy-start(bf16[192,2048]{1,0:T(8,128)(2,1)} %t_hbm.1) | copy-start | bytes 2359300
  1.1 0.9 %copy-start.1 = (bf16[192,512]{1,0:T(8,128)(2,1)S(1)}, bf16[192,512]{1,0:T(8,128)(2,1)}, u32[]{:S(2)}) copy-start(bf16[192,512]{1,0:T(8,128)(2,1)} %s_hbm.1) | copy-start | bytes 589828
